TPU v7x, 32 devices: a whole 2x2x4 slice. The times are simulated.
32 devices in a mesh: wide: 8 (over z, x), narrow: 4 (over y, core).
Axes of the slice: x: 2, y: 2, z: 4, core: 2. Of those that a mesh axis runs over, the one named last changes fastest.
Arguments:
- tokens: bfloat16 [32768, 1024], P(('wide', 'narrow')), may hold values from -6 to 6
- cotangent: bfloat16 [32768, 1024], P(('wide', 'narrow')), may hold values from -6 to 6
- seq_lens: int32 [32, 4], P(('wide', 'narrow')), may hold values from 0 to 1024, as said below
- norm_gain: bfloat16 [1024], P(('wide', 'narrow')), may hold values from 0.099609375 to 1.8984375
- norm_bias: bfloat16 [1024], P(('wide', 'narrow')), may hold values from -4 to 4
- qkv_weight: bfloat16 [1024, 3072], P(('wide', 'narrow')), may hold values from -0.1875 to 0.1875
- qkv_bias: bfloat16 [3072], P(('wide', 'narrow')), may hold values from -4 to 4
- out_weight: bfloat16 [1024, 1024], P(('wide', 'narrow')), may hold values from -3 to 3
- out_bias: bfloat16 [1024], P(('wide', 'narrow')), may hold values from -4 to 4
- fc_in_weight: bfloat16 [1024, 4096], P(('wide', 'narrow')), may hold values from -0.1875 to 0.1875
- fc_in_bias: bfloat16 [4096], P(('wide', 'narrow')), may hold values from -4 to 4
- fc_out_weight: bfloat16 [4096, 1024], P(('wide', 'narrow')), may hold values from -0.09375 to 0.09375
- fc_out_bias: bfloat16 [1024], P(('wide', 'narrow')), may hold values from -4 to 4
Outputs:
- mixed: bfloat16 [32768, 1024], P(('wide', 'narrow'))
- tokens_grad: bfloat16 [32768, 1024], P(('wide', 'narrow'))
- norm_gain_grad: float32 [1024], P(('wide', 'narrow'))
- norm_bias_grad: float32 [1024], P(('wide', 'narrow'))
- qkv_weight_grad: float32 [1024, 3072], P(('wide', 'narrow'))
- qkv_bias_grad: float32 [3072], P(('wide', 'narrow'))
- out_weight_grad: float32 [1024, 1024], P(('wide', 'narrow'))
- out_bias_grad: float32 [1024], P(('wide', 'narrow'))
- fc_in_weight_grad: float32 [1024, 4096], P(('wide', 'narrow'))
- fc_in_bias_grad: float32 [4096], P(('wide', 'narrow'))
- fc_out_weight_grad: float32 [4096, 1024], P(('wide', 'narrow'))
- fc_out_bias_grad: float32 [1024], P(('wide', 'narrow'))
- stream_rms: float32 [32, 3], P(('wide', 'narrow'))
Inputs may be any that keep to these rules, and one draw needn't show every extreme that they name: `seq_lens`: row r lists the sequences packed in order on device r: each length is 1024, half of it or a quarter of it (256), zeros come last, the lengths of a row add up to 1024; in every draw some device holds one single sequence of 1024 tokens.
All inputs are finite; a program needn't handle non-finite values.
Results may differ from a plain program's by a relative error of at most 0.0099.
Values may be sent and summed in bfloat16 or wider, within the bound.
A program may use at most 256 MiB of HBM per device.

v0:
```python
from functools import partial

import jax
import jax.numpy as jnp
from jax import lax
from jax.sharding import PartitionSpec as P

HEADS = 16
HEAD = 64
ROT = 16


epsilon = 1e-05


def positions(lengths, count):
    ends = jnp.cumsum(lengths)
    places = jnp.arange(count, dtype=jnp.int32)
    segment = jnp.sum((places[:, None] >= ends[None, :]).astype(jnp.int32), axis=1)
    starts = ends - lengths
    slots = jnp.arange(lengths.shape[0], dtype=jnp.int32)
    begin = jnp.sum(jnp.where(segment[:, None] == slots[None, :], starts[None, :], 0), axis=1)
    return (segment, places, (places - begin).astype(jnp.float32))


def rotate(vector, cosine, sine):
    half = ROT // 2
    first = vector[..., :half]
    second = vector[..., half:ROT]
    return jnp.concatenate(
        [first * cosine - second * sine, second * cosine + first * sine, vector[..., ROT:]], axis=-1
    )


def unrotate(grad, cosine, sine):
    half = ROT // 2
    first = grad[..., :half]
    second = grad[..., half:ROT]
    return jnp.concatenate(
        [first * cosine + second * sine, second * cosine - first * sine, grad[..., ROT:]], axis=-1
    )


def times_transposed(left, right):
    return lax.dot_general(
        left, right, (((1,), (1,)), ((), ())), preferred_element_type=jnp.float32
    )


def transposed_times(left, right):
    return lax.dot_general(
        left, right, (((0,), (0,)), ((), ())), preferred_element_type=jnp.float32
    )


def block_scores(query_block, key_low, seg_query, seg_key, place_query, place_key):
    raw = jnp.einsum(
        "qhd,khd->hqk", query_block, key_low, preferred_element_type=jnp.float32
    ) * HEAD ** (-0.5)
    allowed = (seg_query[:, None] == seg_key[None, :]) & (
        place_key[None, :] <= place_query[:, None]
    )
    return (jnp.where(allowed[None], raw, -1e30), allowed)


def local(
    tokens,
    cotangent,
    seq_lens,
    norm_gain,
    norm_bias,
    qkv_weight,
    qkv_bias,
    out_weight,
    out_bias,
    fc_in_weight,
    fc_in_bias,
    fc_out_weight,
    fc_out_bias,
):
    shards = (
        norm_gain,
        norm_bias,
        qkv_weight,
        qkv_bias,
        out_weight,
        out_bias,
        fc_in_weight,
        fc_in_bias,
        fc_out_weight,
        fc_out_bias,
    )
    gathered = (
        lax.all_gather(shards[0], ("wide", "narrow"), axis=0, tiled=True),
        lax.all_gather(shards[1], ("wide", "narrow"), axis=0, tiled=True),
        lax.all_gather(shards[2], ("wide", "narrow"), axis=0, tiled=True),
        lax.all_gather(shards[3], ("wide", "narrow"), axis=0, tiled=True),
        lax.all_gather(shards[4], ("wide", "narrow"), axis=0, tiled=True),
        lax.all_gather(shards[5], ("wide", "narrow"), axis=0, tiled=True),
        lax.all_gather(shards[6], ("wide", "narrow"), axis=0, tiled=True),
        lax.all_gather(shards[7], ("wide", "narrow"), axis=0, tiled=True),
        lax.all_gather(shards[8], ("wide", "narrow"), axis=0, tiled=True),
        lax.all_gather(shards[9], ("wide", "narrow"), axis=0, tiled=True),
    )
    gain_full = gathered[0].astype(jnp.float32)
    shift_full = gathered[1].astype(jnp.float32)
    qkv_matrix = gathered[2]
    qkv_offset = gathered[3].astype(jnp.float32)
    out_matrix = gathered[4]
    out_offset = gathered[5].astype(jnp.float32)
    in_matrix = gathered[6]
    in_offset = gathered[7].astype(jnp.float32)
    down_matrix = gathered[8]
    down_offset = gathered[9].astype(jnp.float32)
    row_count = tokens.shape[0]
    width = tokens.shape[1]
    inputs = tokens.astype(jnp.float32)
    centred = inputs - jnp.mean(inputs, axis=-1, keepdims=True)
    inverse = lax.rsqrt(jnp.mean(centred * centred, axis=-1, keepdims=True) + epsilon)
    normed = centred * inverse
    hid_low = (normed * gain_full + shift_full).astype(jnp.bfloat16)
    qkv = jnp.dot(hid_low, qkv_matrix, preferred_element_type=jnp.float32) + qkv_offset
    segment, places, offset = positions(seq_lens[0], row_count)
    freqs = 10000.0 ** (-jnp.arange(ROT // 2, dtype=jnp.float32) * 2.0 / ROT)
    angle = offset[:, None] * freqs[None, :]
    cosine = jnp.cos(angle)[:, None, :]
    sine = jnp.sin(angle)[:, None, :]
    q_low = rotate(qkv[:, :width].reshape(row_count, HEADS, HEAD), cosine, sine).astype(
        jnp.bfloat16
    )
    k_low = rotate(qkv[:, width : 2 * width].reshape(row_count, HEADS, HEAD), cosine, sine).astype(
        jnp.bfloat16
    )
    v_low = qkv[:, 2 * width :].reshape(row_count, HEADS, HEAD).astype(jnp.bfloat16)
    block_rows = min(512, row_count)
    block_count = row_count // block_rows
    outputs = []
    kept_lse = []
    for block in range(block_count):
        lower = block * block_rows
        upper = lower + block_rows
        scores, allowed = block_scores(
            q_low[lower:upper],
            k_low[:upper],
            segment[lower:upper],
            segment[:upper],
            places[lower:upper],
            places[:upper],
        )
        row_max = jnp.max(scores, axis=-1, keepdims=True)
        expo = jnp.exp(scores - row_max)
        totals = jnp.sum(expo, axis=-1, keepdims=True)
        soft_low = (expo / totals).astype(jnp.bfloat16)
        kept_lse.append(row_max + jnp.log(totals))
        outputs.append(
            jnp.einsum("hqk,khd->qhd", soft_low, v_low[:upper], preferred_element_type=jnp.float32)
        )
    att_low = jnp.concatenate(outputs, axis=0).reshape(row_count, width).astype(jnp.bfloat16)
    attn_out = jnp.dot(att_low, out_matrix, preferred_element_type=jnp.float32) + out_offset
    pre = jnp.dot(hid_low, in_matrix, preferred_element_type=jnp.float32) + in_offset
    gelu_exact = partial(jax.nn.gelu, approximate=False)
    act_low = gelu_exact(pre).astype(jnp.bfloat16)
    mlp = jnp.dot(act_low, down_matrix, preferred_element_type=jnp.float32) + down_offset
    mixed = (inputs + attn_out + mlp).astype(jnp.bfloat16)
    stream_rms = jnp.sqrt(
        jnp.stack([jnp.mean(inputs * inputs), jnp.mean(attn_out * attn_out), jnp.mean(mlp * mlp)])
    )[None, :]
    regathered = (
        lax.all_gather(shards[0], ("wide", "narrow"), axis=0, tiled=True),
        lax.all_gather(shards[1], ("wide", "narrow"), axis=0, tiled=True),
        lax.all_gather(shards[2], ("wide", "narrow"), axis=0, tiled=True),
        lax.all_gather(shards[3], ("wide", "narrow"), axis=0, tiled=True),
        lax.all_gather(shards[4], ("wide", "narrow"), axis=0, tiled=True),
        lax.all_gather(shards[5], ("wide", "narrow"), axis=0, tiled=True),
        lax.all_gather(shards[6], ("wide", "narrow"), axis=0, tiled=True),
        lax.all_gather(shards[7], ("wide", "narrow"), axis=0, tiled=True),
        lax.all_gather(shards[8], ("wide", "narrow"), axis=0, tiled=True),
        lax.all_gather(shards[9], ("wide", "narrow"), axis=0, tiled=True),
    )
    gain_back = regathered[0].astype(jnp.float32)
    qkv_back = regathered[2]
    out_back = regathered[4]
    in_back = regathered[6]
    down_back = regathered[8]
    upstream = cotangent.astype(jnp.float32)
    grad_down_matrix = transposed_times(act_low, cotangent)
    grad_down_offset = jnp.sum(upstream, axis=0)
    grad_out_matrix = transposed_times(att_low, cotangent)
    grad_out_offset = jnp.sum(upstream, axis=0)
    act_grad = times_transposed(cotangent, down_back)
    _, gelu_pull = jax.vjp(gelu_exact, pre)
    pre_grad_low = gelu_pull(act_grad)[0].astype(jnp.bfloat16)
    grad_in_matrix = transposed_times(hid_low, pre_grad_low)
    grad_in_offset = jnp.sum(pre_grad_low.astype(jnp.float32), axis=0)
    att_grad_low = (
        times_transposed(cotangent, out_back).astype(jnp.bfloat16).reshape(row_count, HEADS, HEAD)
    )
    query_grads = []
    key_grad = jnp.zeros((row_count, HEADS, HEAD), jnp.float32)
    value_grad = jnp.zeros((row_count, HEADS, HEAD), jnp.float32)
    for block in range(block_count):
        lower = block * block_rows
        upper = lower + block_rows
        query_block = q_low[lower:upper]
        scores, allowed = block_scores(
            query_block,
            k_low[:upper],
            segment[lower:upper],
            segment[:upper],
            places[lower:upper],
            places[:upper],
        )
        soft = jnp.where(allowed[None], jnp.exp(scores - kept_lse[block]), 0.0)
        soft_low = soft.astype(jnp.bfloat16)
        out_grad = att_grad_low[lower:upper]
        value_part = jnp.einsum(
            "hqk,qhd->khd", soft_low, out_grad, preferred_element_type=jnp.float32
        )
        prob_grad = jnp.einsum(
            "qhd,khd->hqk", out_grad, v_low[:upper], preferred_element_type=jnp.float32
        )
        score_grad = soft * (prob_grad - jnp.sum(soft * prob_grad, axis=-1, keepdims=True))
        score_low = score_grad.astype(jnp.bfloat16)
        query_grads.append(
            jnp.einsum("hqk,khd->qhd", score_low, k_low[:upper], preferred_element_type=jnp.float32)
            * HEAD ** (-0.5)
        )
        key_part = jnp.einsum(
            "hqk,qhd->khd", score_low, query_block, preferred_element_type=jnp.float32
        ) * HEAD ** (-0.5)
        padding = ((0, row_count - upper), (0, 0), (0, 0))
        key_grad = key_grad + jnp.pad(key_part, padding)
        value_grad = value_grad + jnp.pad(value_part, padding)
    query_grad = unrotate(jnp.concatenate(query_grads, axis=0), cosine, sine)
    key_grad = unrotate(key_grad, cosine, sine)
    qkv_grad_low = jnp.concatenate(
        [
            query_grad.reshape(row_count, width),
            key_grad.reshape(row_count, width),
            value_grad.reshape(row_count, width),
        ],
        axis=1,
    ).astype(jnp.bfloat16)
    grad_qkv_matrix = transposed_times(hid_low, qkv_grad_low)
    grad_qkv_offset = jnp.sum(qkv_grad_low.astype(jnp.float32), axis=0)
    hidden_grad = times_transposed(qkv_grad_low, qkv_back) + times_transposed(pre_grad_low, in_back)
    grad_gain = jnp.sum(hidden_grad * normed, axis=0)
    grad_shift = jnp.sum(hidden_grad, axis=0)
    scaled = hidden_grad * gain_back
    input_grad = upstream + inverse * (
        scaled
        - jnp.mean(scaled, axis=-1, keepdims=True)
        - normed * jnp.mean(scaled * normed, axis=-1, keepdims=True)
    )
    tokens_grad = input_grad.astype(jnp.bfloat16)
    summed = (
        lax.psum_scatter(grad_gain, ("wide", "narrow"), scatter_dimension=0, tiled=True),
        lax.psum_scatter(grad_shift, ("wide", "narrow"), scatter_dimension=0, tiled=True),
        lax.psum_scatter(grad_qkv_matrix, ("wide", "narrow"), scatter_dimension=0, tiled=True),
        lax.psum_scatter(grad_qkv_offset, ("wide", "narrow"), scatter_dimension=0, tiled=True),
        lax.psum_scatter(grad_out_matrix, ("wide", "narrow"), scatter_dimension=0, tiled=True),
        lax.psum_scatter(grad_out_offset, ("wide", "narrow"), scatter_dimension=0, tiled=True),
        lax.psum_scatter(grad_in_matrix, ("wide", "narrow"), scatter_dimension=0, tiled=True),
        lax.psum_scatter(grad_in_offset, ("wide", "narrow"), scatter_dimension=0, tiled=True),
        lax.psum_scatter(grad_down_matrix, ("wide", "narrow"), scatter_dimension=0, tiled=True),
        lax.psum_scatter(grad_down_offset, ("wide", "narrow"), scatter_dimension=0, tiled=True),
    )
    return (
        mixed,
        tokens_grad,
        summed[0],
        summed[1],
        summed[2],
        summed[3],
        summed[4],
        summed[5],
        summed[6],
        summed[7],
        summed[8],
        summed[9],
        stream_rms,
    )


def solution(mesh):
    return jax.shard_map(
        local,
        mesh=mesh,
        in_specs=(
            P(("wide", "narrow"), None),
            P(("wide", "narrow"), None),
            P(("wide", "narrow"), None),
            P(("wide", "narrow")),
            P(("wide", "narrow")),
            P(("wide", "narrow"), None),
            P(("wide", "narrow")),
            P(("wide", "narrow"), None),
            P(("wide", "narrow")),
            P(("wide", "narrow"), None),
            P(("wide", "narrow")),
            P(("wide", "narrow"), None),
            P(("wide", "narrow")),
        ),
        out_specs=(
            P(("wide", "narrow"), None),
            P(("wide", "narrow"), None),
            P(("wide", "narrow")),
            P(("wide", "narrow")),
            P(("wide", "narrow"), None),
            P(("wide", "narrow")),
            P(("wide", "narrow"), None),
            P(("wide", "narrow")),
            P(("wide", "narrow"), None),
            P(("wide", "narrow")),
            P(("wide", "narrow"), None),
            P(("wide", "narrow")),
            P(("wide", "narrow"), None),
        ),
        check_vma=False,
    )
```

profile of v0, /device:TPU:0, one launch (start us, length us, event | category | flops | bytes accessed | tf_op | source)
XLA Modules:
  0.0 981.2 jit_solution(13516515181250752874)
XLA Ops:
  20.2 42.4 %all-reduce.13 = (bf16[1024]{0:T(1024)(128)(2,1)S(1)}, bf16[1024]{0:T(1024)(128)(2,1)S(1)}, bf16[3072]{0:T(1024)(128)(2,1)S(1)}, bf16[1024]{0:T(1024)(128)(2,1)}, bf16[1024]{0:T(1024)(128)(2,1)}) all-reduce(bf16[1024]{0:T(1024)(128)(2,1)S(1)} %dynamic-update-slice.1, ...), channel_id=1, replica_groups=mesh['wide'=8,'narrow'=4] {'wide','narrow'}, use_global_device_ids=true, to_apply=%add.3 | all-reduce | flops 7168 | bytes 28672
  62.7 40.7 %all-gather = bf16[32,1,128]{2,1,0:T(2,128)(2,1)S(1)} all-gather(bf16[1,1,128]{2,1,0:T(2,128)(2,1)} %bitcast.96), channel_id=1, replica_groups=mesh['wide'=8,'narrow'=4] {'wide','narrow'}, dimensions={0}, use_global_device_ids=true | all-gather | bytes 8448 | tf_op jit(solution)/shard_map/all_gather | solution.py:101
  111.4 30.5 %all-gather.6.cloned.1.call-done = bf16[1024,3072]{1,0:T(8,128)(2,1)} async-done(((bf16[32,3072]{1,0:T(8,128)(2,1)}), bf16[1024,3072]{1,0:T(8,128)(2,1)}) %all-gather.6.cloned.1.call-update) | async-done | bytes 6291472 | tf_op jit(solution)/shard_map/all_gather | solution.py:96
  186.5 10.3 %fusion.11 = f32[16,512]{1,0:T(8,128)S(1)} fusion(f32[16,512,512]{1,2,0:T(8,128)} %get-tuple-element.61, f32[16,512]{1,0:T(8,128)S(1)} %get-tuple-element.60, pred[512,512]{0,1:T(8,128)(4,1)S(1)} %compare_and_fusion), kind=kLoop, calls=%fused_computation.35 | loop fusion | flops 16769024 | bytes 17104896 | tf_op jit(solution)/shard_map/reduce_sum | solution.py:152
  196.8 16.0 %fusion.1 = (f32[16,512]{1,0:T(8,128)S(1)}, f32[16,512,1024]{2,1,0:T(8,128)}) fusion(pred[512,1024]{1,0:T(8,128)(4,1)S(1)} %fusion.37, bf16[1024,16,48]{0,2,1:T(8,128)(2,1)S(1)} %slice.204, bf16[1024,16,8]{0,2,1:T(8,128)(2,1)S(1)} %get-tuple-element.38, bf16[1024,16,8]{0,2,1:T(8,128)(2,1)S(1)} %get-tuple-element.37, bf16[1024,16,64]{0,2,1:T(8,128)(2,1)} %copy-done.5), kind=kOutput, calls=%fused_computation.8 | convolution fusion | flops 1105190912 | bytes 37257216 | tf_op jit(solution)/shard_map/qhd,khd->hqk/dot_general | solution.py:57
  212.9 15.2 %fusion = f32[16,512]{1,0:T(8,128)S(1)} fusion(f32[16,512,1024]{2,1,0:T(8,128)} %get-tuple-element.59, f32[16,512]{1,0:T(8,128)S(1)} %get-tuple-element.58, pred[512,1024]{1,0:T(8,128)(4,1)S(1)} %fusion.37), kind=kLoop, calls=%fused_computation.6 | loop fusion | flops 33546240 | bytes 34144256 | tf_op jit(solution)/shard_map/reduce_sum | solution.py:152
  236.9 14.6 %fusion.43 = bf16[512,16,64]{0,2,1:T(8,128)(2,1)S(1)} fusion(bf16[1024,16,64]{0,2,1:T(8,128)(2,1)S(1)} %bitcast.87, f32[16,512,1024]{2,1,0:T(8,128)} %get-tuple-element.59, f32[16,512]{1,0:T(8,128)S(1)} %fusion, f32[16,512]{1,0:T(8,128)S(1)} %get-tuple-element.58, pred[512,1024]{1,0:T(8,128)(4,1)S(1)} %fusion.37), kind=kOutput, calls=%fused_computation.96 | convolution fusion | flops 1116209152 | bytes 37289984 | tf_op jit(solution)/shard_map/hqk,khd->qhd/dot_general | solution.py:156
  257.4 12.5 %multiply_reduce_fusion.1 = (f32[16,512]{1,0:T(8,128)S(1)}, f32[16,512,512]{1,2,0:T(8,128)}) fusion(f32[16,512]{1,0:T(8,128)S(1)} %log_add_fusion.1, f32[16,512,512]{1,2,0:T(8,128)} %get-tuple-element.61, pred[512,512]{0,1:T(8,128)(4,1)S(1)} %compare_and_fusion, bf16[512,16,64]{0,2,1:T(8,128)(2,1)S(1)} %bitcast.92, bf16[512,16,64]{0,2,1:T(8,128)(2,1)S(1)} %bitcast.89), kind=kOutput, calls=%fused_computation.15 | convolution fusion | flops 562028544 | bytes 35979264 | tf_op jit(solution)/shard_map/qhd,khd->hqk/dot_general | solution.py:219
  269.9 12.9 %multiply_convert_fusion.1 = bf16[16,512,512]{1,2,0:T(8,128)(2,1)S(1)} fusion(f32[16,512,512]{1,2,0:T(8,128)} %get-tuple-element.63, f32[16,512]{1,0:T(8,128)S(1)} %get-tuple-element.62, f32[16,512]{1,0:T(8,128)S(1)} %log_add_fusion.1, f32[16,512,512]{1,2,0:T(8,128)} %get-tuple-element.61, pred[512,512]{0,1:T(8,128)(4,1)S(1)} %compare_and_fusion), kind=kLoop, calls=%fused_computation.14 | loop fusion | flops 29360128 | bytes 42270720 | tf_op jit(solution)/shard_map/convert_element_type | solution.py:223
  290.1 27.1 %multiply_reduce_fusion = (f32[16,512]{1,0:T(8,128)S(1)}, f32[16,512,1024]{2,1,0:T(8,128)}) fusion(f32[16,512]{1,0:T(8,128)S(1)} %log_add_fusion, f32[16,512,1024]{2,1,0:T(8,128)} %get-tuple-element.59, pred[512,1024]{1,0:T(8,128)(4,1)S(1)} %fusion.37, bf16[512,16,64]{0,2,1:T(8,128)(2,1)} %bitcast.90, bf16[1024,16,64]{0,2,1:T(8,128)(2,1)} %bitcast.86), kind=kOutput, calls=%fused_computation.1 | convolution fusion | flops 1124065280 | bytes 70844416 | tf_op jit(solution)/shard_map/qhd,khd->hqk/dot_general | solution.py:219
  317.2 28.2 %multiply_convert_fusion = bf16[16,512,1024]{2,1,0:T(8,128)(2,1)} fusion(f32[16,512,1024]{2,1,0:T(8,128)} %get-tuple-element.65, f32[16,512]{1,0:T(8,128)S(1)} %get-tuple-element.64, f32[16,512]{1,0:T(8,128)S(1)} %log_add_fusion, f32[16,512,1024]{2,1,0:T(8,128)} %get-tuple-element.59, pred[512,1024]{1,0:T(8,128)(4,1)S(1)} %fusion.37), kind=kLoop, calls=%fused_computation | loop fusion | flops 58720256 | bytes 84475904 | tf_op jit(solution)/shard_map/convert_element_type | solution.py:223
  363.4 12.9 %multiply_bitcast_fusion.1 = f32[512,16,64]{0,2,1:T(8,128)} fusion(bf16[16,512,1024]{2,1,0:T(8,128)(2,1)} %multiply_convert_fusion, bf16[1024,16,48]{0,2,1:T(8,128)(2,1)} %copy-done.3, bf16[1024,16,8]{0,2,1:T(8,128)(2,1)S(1)} %copy-done.17, bf16[1024,16,8]{0,2,1:T(8,128)(2,1)S(1)} %copy-done.15), kind=kOutput, calls=%fused_computation.87 | convolution fusion | flops 1080557568 | bytes 20971520 | tf_op jit(solution)/shard_map/hqk,khd->qhd/dot_general | solution.py:225
  391.6 18.4 %fusion.33 = bf16[1024,16,64]{0,2,1:T(8,128)(2,1)} fusion(f32[512,16,64]{0,2,1:T(8,128)} %fusion.38, bf16[512,16,64]{0,2,1:T(8,128)(2,1)} %bitcast.91, f32[16,512]{1,0:T(8,128)S(1)} %log_add_fusion, f32[16,512,1024]{2,1,0:T(8,128)} %get-tuple-element.59, pred[512,1024]{1,0:T(8,128)(4,1)S(1)} %fusion.37), kind=kOutput, calls=%fused_computation.71 | convolution fusion | flops 1117782016 | bytes 39354368 | tf_op jit(solution)/shard_map/hqk,qhd->khd/dot_general | solution.py:216
  410.1 14.6 %fusion.66 = f32[1024,3072]{1,0:T(8,128)} fusion(bf16[1024,1024]{0,1:T(8,128)(2,1)} %bitcast.83, bf16[1024,1024]{0,1:T(8,128)(2,1)} %bitcast.78, bf16[1024,1024]{0,1:T(8,128)(2,1)} %bitcast.75, bf16[1024,1024]{1,0:T(8,128)(2,1)S(1)} %copy-done.9, f32[1024]{0:T(1024)S(1)} %copy-done.37, f32[1024]{0:T(1024)S(1)} %copy-done.34, f32[1024]{0:T(1024)S(1)} %copy-done.40, ...), kind=kOutput, calls=%fused_computation.145 | convolution fusion | flops 6467616768 | bytes 20987904 | tf_op jit(solution)/shard_map/dot_general | solution.py:51
  424.7 15.1 %fusion.71 = f32[1024,4096]{1,0:T(8,128)} fusion(bf16[1024,4096]{1,0:T(8,128)(2,1)} %all-gather.10.cloned.1.call-done, bf16[1024,1024]{1,0:T(8,128)(2,1)S(1)} %copy-done.9, f32[1024]{0:T(1024)S(1)} %copy-done.37, f32[1024]{0:T(1024)S(1)} %copy-done.34, f32[1024]{0:T(1024)S(1)} %copy-done.40, f32[1024]{0:T(1024)S(1)} %copy-done.31), kind=kOutput, calls=%fused_computation.148 | convolution fusion | flops 8596226048 | bytes 27279360 | tf_op jit(solution)/shard_map/dot_general | solution.py:160
  439.9 51.2 %convert_reduce_fusion = (f32[4096]{0:T(1024)S(1)}, bf16[1024,4096]{1,0:T(8,128)(2,1)}, f32[1024,4096]{1,0:T(8,128)S(1)}) fusion(f32[1024,4096]{1,0:T(8,128)} %fusion.71, f32[4096]{0:T(1024)S(1)} %bitcast.94, bf16[1024,1024]{1,0:T(8,128)(2,1)} %param.14, bf16[4096,1024]{1,0:T(8,128)(2,1)} %all-gather.12.cloned.1.call-done), kind=kOutput, calls=%fused_computation.10 | convolution fusion | flops 8904503296 | bytes 52461568 | tf_op jit(solution)/shard_map/dot_general | solution.py:45
  503.3 11.7 %fusion.81 = f32[4096,1024]{1,0:T(8,128)} fusion(bf16[1024,4096]{1,0:T(8,128)(2,1)S(1)} %multiply_convert_fusion.2, bf16[1024,1024]{1,0:T(8,128)(2,1)S(1)} %copy-done.45), kind=kOutput, calls=%fused_computation.155 | convolution fusion | flops 8589934592 | bytes 27262976 | tf_op jit(solution)/shard_map/dot_general | solution.py:51
  516.6 15.4 %fusion.68 = f32[1024,4096]{1,0:T(8,128)} fusion(bf16[1024,4096]{1,0:T(8,128)(2,1)} %get-tuple-element.29, bf16[1024,1024]{1,0:T(8,128)(2,1)S(1)} %copy-done.10, f32[1024]{0:T(1024)S(1)} %copy-done.38, f32[1024]{0:T(1024)S(1)} %copy-done.35, f32[1024]{0:T(1024)S(1)} %copy-done.41, f32[1024]{0:T(1024)S(1)} %copy-done.32), kind=kOutput, calls=%fused_computation.147 | convolution fusion | flops 8596226048 | bytes 27279360 | tf_op jit(solution)/shard_map/dot_general | solution.py:51
  537.7 9.7 fusion.67
  547.5 17.8 %fusion.27 = (f32[1024]{0:T(1024)S(1)}, f32[1024]{0:T(1024)S(1)}, f32[1024]{0:T(1024)S(1)}, f32[1024]{0:T(1024)S(1)}, f32[]{:T(128)}, /*index=5*/f32[1024,1024]{1,0:T(8,128)}) fusion(bf16[1024,1024]{1,0:T(8,128)(2,1)S(1)} %copy-done.10, f32[1024]{0:T(1024)S(1)} %copy-done.41, f32[1024]{0:T(1024)S(1)} %copy-done.32, f32[1024]{0:T(1024)S(1)} %copy-done.35, ...), kind=kOutput, calls=%fused_computation.64 | convolution fusion | flops 8603561984 | bytes 27291652 | tf_op jit(solution)/shard_map/dot_general | solution.py:45
  566.0 12.7 %fusion.79 = f32[1024,1024]{1,0:T(8,128)S(1)} fusion(bf16[1024,4096]{1,0:T(8,128)(2,1)} %copy-done.7, bf16[4096,1024]{1,0:T(8,128)(2,1)} %all-gather.12.cloned.1.call-done), kind=kOutput, calls=%fused_computation.153 | convolution fusion | flops 8589934592 | bytes 20971520 | tf_op jit(solution)/shard_map/dot_general | solution.py:163
  586.8 42.0 %all-reduce.12 = (f32[1024]{0:T(1024)S(1)}, f32[1024]{0:T(1024)S(1)}, f32[3072]{0:T(1024)S(1)}, f32[1024]{0:T(1024)S(1)}, f32[4096]{0:T(1024)S(1)}) all-reduce(f32[1024]{0:T(1024)S(1)} %get-tuple-element.13, f32[1024]{0:T(1024)S(1)} %get-tuple-element.16, ...), channel_id=2, replica_groups=mesh['wide'=8,'narrow'=4] {'wide','narrow'}, use_global_device_ids=true, to_apply=%region_14.15.clone | all-reduce | flops 10240 | bytes 81920
  631.8 154.3 %reduce-scatter.11.cloned.1.call-done = f32[128,1024]{1,0:T(8,128)} async-done(((f32[4096,1024]{1,0:T(8,128)}), f32[128,1024]{1,0:T(8,128)}) %reduce-scatter.11.cloned.1.call-update) | async-done | bytes 524304 | tf_op jit(solution)/shard_map/reduce_scatter | solution.py:265
  786.2 187.5 %reduce-scatter.9.cloned.1.call-done = f32[32,4096]{1,0:T(8,128)} async-done(((f32[1024,4096]{1,0:T(8,128)}), f32[32,4096]{1,0:T(8,128)}) %reduce-scatter.9.cloned.1.call-update) | async-done | bytes 524304 | tf_op jit(solution)/shard_map/reduce_scatter | solution.py:263
  (195 shorter events, 150.4 us)
Async XLA Ops:
  7.2 97.9 %all-gather.8.cloned.1.call-start = ((), (), s32[]{:S(2)}) async-start(), calls=%async_computation.5 | async-start | bytes 2162688 | tf_op jit(solution)/shard_map/all_gather | solution.py:98
  7.9 134.0 %all-gather.6.cloned.1.call-start = ((), (), s32[]{:S(2)}) async-start(), calls=%async_computation.4 | async-start | bytes 6488064 | tf_op jit(solution)/shard_map/all_gather | solution.py:96
  8.7 416.1 %all-gather.10.cloned.1.call-start = ((), (), s32[]{:S(2)}) async-start(), calls=%async_computation.6 | async-start | bytes 8650752 | tf_op jit(solution)/shard_map/all_gather | solution.py:100
  9.4 430.5 %all-gather.12.cloned.1.call-start = ((), (), s32[]{:S(2)}) async-start(), calls=%async_computation.7 | async-start | bytes 8650752 | tf_op jit(solution)/shard_map/all_gather | solution.py:102
  10.0 621.9 %reduce-scatter.7.cloned.1.call-start = ((), (), s32[]{:S(2)}) async-start(), calls=%async_computation.9 | async-start | bytes 4325376 | tf_op jit(solution)/shard_map/reduce_scatter | solution.py:261
  13.7 128.2 %copy-start.30 = (f32[1024]{0:T(1024)}, f32[1024]{0:T(1024)S(1)}, u32[]{:S(2)}) copy-start(f32[1024]{0:T(1024)S(1)} %broadcast_multiply_fusion.2) | copy-start | bytes 12292
  16.0 125.9 %copy-start.39 = (f32[1024]{0:T(1024)}, f32[1024]{0:T(1024)S(1)}, u32[]{:S(2)}) copy-start(f32[1024]{0:T(1024)S(1)} %add_rsqrt_fusion) | copy-start | bytes 12292
  62.6 79.3 %copy-start.36 = (f32[1024]{0:T(1024)}, f32[1024]{0:T(1024)S(1)}, u32[]{:S(2)}) copy-start(f32[1024]{0:T(1024)S(1)} %convert_element_type.93) | copy-start | bytes 12292
  62.6 79.3 %copy-start.33 = (f32[1024]{0:T(1024)}, f32[1024]{0:T(1024)S(1)}, u32[]{:S(2)}) copy-start(f32[1024]{0:T(1024)S(1)} %convert_element_type.92) | copy-start | bytes 12292
  104.1 72.8 %copy-start.25 = (f32[1024,8]{0,1:T(8,128)}, f32[1024,8]{0,1:T(8,128)S(1)}, u32[]{:S(2)}) copy-start(f32[1024,8]{0,1:T(8,128)S(1)} %get-tuple-element.52) | copy-start | bytes 98308
  104.2 72.8 %copy-start.27 = (f32[1024,8]{0,1:T(8,128)}, f32[1024,8]{0,1:T(8,128)S(1)}, u32[]{:S(2)}) copy-start(f32[1024,8]{0,1:T(8,128)S(1)} %get-tuple-element.53) | copy-start | bytes 98308
  105.0 36.9 %copy-start.8 = (bf16[1024,1024]{1,0:T(8,128)(2,1)S(1)}, bf16[1024,1024]{1,0:T(8,128)(2,1)}, u32[]{:S(2)}) copy-start(bf16[1024,1024]{1,0:T(8,128)(2,1)} %param.13) | copy-start | bytes 6291460
  168.9 27.9 %copy-start.3 = (bf16[1024,16,48]{0,2,1:T(8,128)(2,1)}, bf16[1024,16,48]{0,2,1:T(8,128)(2,1)S(1)}, u32[]{:S(2)}) copy-start(bf16[1024,16,48]{0,2,1:T(8,128)(2,1)S(1)} %slice.204) | copy-start | bytes 4718596
  178.8 18.0 %copy-start.14 = (bf16[1024,16,8]{0,2,1:T(8,128)(2,1)}, bf16[1024,16,8]{0,2,1:T(8,128)(2,1)S(1)}, u32[]{:S(2)}) copy-start(bf16[1024,16,8]{0,2,1:T(8,128)(2,1)S(1)} %get-tuple-element.37) | copy-start | bytes 786436
  178.8 18.0 %copy-start.16 = (bf16[1024,16,8]{0,2,1:T(8,128)(2,1)}, bf16[1024,16,8]{0,2,1:T(8,128)(2,1)S(1)}, u32[]{:S(2)}) copy-start(bf16[1024,16,8]{0,2,1:T(8,128)(2,1)S(1)} %get-tuple-element.38) | copy-start | bytes 786436
  290.0 341.8 %reduce-scatter.5.cloned.1.call-start = ((), (), s32[]{:S(2)}) async-start(), calls=%async_computation.8 | async-start | bytes 12976128 | tf_op jit(solution)/shard_map/reduce_scatter | solution.py:259
  391.6 18.4 %copy-start.9 = (bf16[1024,1024]{1,0:T(8,128)(2,1)S(1)}, bf16[1024,1024]{1,0:T(8,128)(2,1)}, u32[]{:S(2)}) copy-start(bf16[1024,1024]{1,0:T(8,128)(2,1)} %param.13) | copy-start | bytes 6291460
  391.6 18.4 %copy-start.31 = (f32[1024]{0:T(1024)S(1)}, f32[1024]{0:T(1024)}, u32[]{:S(2)}) copy-start(f32[1024]{0:T(1024)} %copy-done.30) | copy-start | bytes 12292
  391.6 18.4 %copy-start.34 = (f32[1024]{0:T(1024)S(1)}, f32[1024]{0:T(1024)}, u32[]{:S(2)}) copy-start(f32[1024]{0:T(1024)} %copy-done.33) | copy-start | bytes 12292
  391.6 18.4 %copy-start.37 = (f32[1024]{0:T(1024)S(1)}, f32[1024]{0:T(1024)}, u32[]{:S(2)}) copy-start(f32[1024]{0:T(1024)} %copy-done.36) | copy-start | bytes 12292
  391.6 18.4 %copy-start.40 = (f32[1024]{0:T(1024)S(1)}, f32[1024]{0:T(1024)}, u32[]{:S(2)}) copy-start(f32[1024]{0:T(1024)} %copy-done.39) | copy-start | bytes 12292
  424.7 361.5 %reduce-scatter.11.cloned.1.call-start = ((), (), s32[]{:S(2)}) async-start(), calls=%async_computation.11 | async-start | bytes 17301504 | tf_op jit(solution)/shard_map/reduce_scatter | solution.py:265
  515.0 458.7 %reduce-scatter.9.cloned.1.call-start = ((), (), s32[]{:S(2)}) async-start(), calls=%async_computation.10 | async-start | bytes 17301504 | tf_op jit(solution)/shard_map/reduce_scatter | solution.py:263
  629.5 344.7 %copy-start.48 = (f32[32]{0:T(128)}, f32[32]{0:T(128)S(1)}, u32[]{:S(2)}) copy-start(f32[32]{0:T(128)S(1)} %dynamic-slice.3) | copy-start | bytes 388
  (34 other events, 261.8 us)
Sparse Core Ops, SparseCore 0:
  10.9 59.5 all-gather.7
  73.3 68.5 all-gather.5
  144.8 76.0 all-gather.9
  223.6 76.1 all-gather.11
  302.5 139.9 reduce-scatter.6
  448.9 151.2 reduce-scatter.4
  603.2 182.9 reduce-scatter.10
  789.1 184.4 reduce-scatter.8
where the time goes:
time: 988 us; the launch traced here: 981 us
  waiting for transfers between devices  375 us (38%)
  matrix products  319 us (32%)
  blocking collectives  125 us (13%)
  other arithmetic  96 us (10%)
  local copies, waits for them, and re-layouts  48.8 us (5%)
  between operations  17 us (2%)
    reduce_scatter x1, waiting for transfers between devices, local(): lax.psum_scatter(grad_in_matrix, ('wide', 'narrow'), scatter_dimension=0,...  187 us
    reduce_scatter x1, waiting for transfers between devices, local(): lax.psum_scatter(grad_down_matrix, ('wide', 'narrow'), scatter_dimension=...  154 us
    unnamed x2, blocking collectives  84.4 us
    dot_general x4, matrix products, times_transposed(): lax.dot_general(left, right, (((1,), (1,)), ((), ())), preferred_element_...  83.5 us
    dot_general x4, matrix products, transposed_times(): lax.dot_general(left, right, (((0,), (0,)), ((), ())), preferred_element_...  46 us
    convert_element_type x2, other arithmetic, local(): score_low = score_grad.astype(jnp.bfloat16)  41 us
    all_gather x1, blocking collectives, local(): lax.all_gather(shards[7], ('wide', 'narrow'), axis=0, tiled=True)  40.7 us
    dot_general x2, matrix products, local(): jnp.einsum('qhd,khd->hqk', out_grad, v_low[:upper], preferred_element_typ...  39.6 us
  transfers between devices with their start and end apart: 8, of which 3 were waited for; matrix products, arithmetic and copies ran while one was open for 46% of the time, Pallas kernels for 0%

commit v1 on v0

v1 whole, which is shorter than its diff:
```python
from functools import partial

import jax
import jax.numpy as jnp
from jax import lax
from jax.experimental import pallas as pl
from jax.experimental.pallas import tpu as pltpu
from jax.sharding import PartitionSpec as P

HEADS = 16
HEAD = 64
ROT = 16
MESH = pl.DeviceIdType.MESH
bf16 = jnp.bfloat16
f32 = jnp.float32
ALL = slice(None)

epsilon = 1e-05


def positions(lengths, count):
    ends = jnp.cumsum(lengths)
    places = jnp.arange(count, dtype=jnp.int32)
    segment = jnp.sum((places[:, None] >= ends[None, :]).astype(jnp.int32), axis=1)
    starts = ends - lengths
    slots = jnp.arange(lengths.shape[0], dtype=jnp.int32)
    begin = jnp.sum(jnp.where(segment[:, None] == slots[None, :], starts[None, :], 0), axis=1)
    return (segment, places, (places - begin).astype(jnp.float32))


def rotate(vector, cosine, sine):
    half = ROT // 2
    first = vector[..., :half]
    second = vector[..., half:ROT]
    return jnp.concatenate(
        [first * cosine - second * sine, second * cosine + first * sine, vector[..., ROT:]], axis=-1
    )


def unrotate(grad, cosine, sine):
    half = ROT // 2
    first = grad[..., :half]
    second = grad[..., half:ROT]
    return jnp.concatenate(
        [first * cosine + second * sine, second * cosine - first * sine, grad[..., ROT:]], axis=-1
    )


def times_transposed(left, right):
    return lax.dot_general(
        left, right, (((1,), (1,)), ((), ())), preferred_element_type=jnp.float32
    )


def transposed_times(left, right):
    return lax.dot_general(
        left, right, (((0,), (0,)), ((), ())), preferred_element_type=jnp.float32
    )


def block_scores(query_block, key_low, seg_query, seg_key, place_query, place_key):
    raw = jnp.einsum(
        "qhd,khd->hqk", query_block, key_low, preferred_element_type=jnp.float32
    ) * HEAD ** (-0.5)
    allowed = (seg_query[:, None] == seg_key[None, :]) & (
        place_key[None, :] <= place_query[:, None]
    )
    return (jnp.where(allowed[None], raw, -1e30), allowed)


QG = 4
MC = 8


class Place:
    def __init__(self):
        wide, narrow = lax.axis_index("wide"), lax.axis_index("narrow")
        self.z, self.x = wide // 2, wide % 2
        self.y, self.c = narrow // 2, narrow % 2
        self.me = (self.z, self.x, self.y, self.c)
        self.zs = [(self.z + d) % 4 for d in (1, 2, 3)]

    def device(self, z, x, y, c):
        return (z * 2 + x, y * 2 + c)

    def partners(self):
        z, x, y, c = self.me
        return [self.device(p, x, y, c) for p in self.zs] + [
            self.device(z, 1 - x, y, c),
            self.device(z, x, 1 - y, c),
            self.device(z, x, y, 1 - c),
        ]

    def greet(self):
        barrier = pltpu.get_barrier_semaphore()
        for other in self.partners():
            pl.semaphore_signal(barrier, inc=1, device_id=other, device_id_type=MESH)
        pl.semaphore_wait(barrier, 6)


class Gather:
    def __init__(self, place, view, x_first, send, recv):
        self.p, self.view, self.x_first, self.send, self.recv = place, view, x_first, send, recv
        self.started = []

    def _copy(self, part, device, slot):
        copy = pltpu.make_async_remote_copy(
            src_ref=self.view(*part),
            dst_ref=self.view(*part),
            send_sem=self.send(slot),
            recv_sem=self.recv(slot),
            device_id=device,
            device_id_type=MESH,
        )
        copy.start()
        self.started.append(copy)
        return copy

    def along_z(self):
        z, x, y, c = self.p.me
        self.waiting = [
            self._copy(self.p.me, self.p.device(other, x, y, c), i)
            for i, other in enumerate(self.p.zs)
        ]

    def arrived(self):
        for copy in self.waiting:
            copy.wait_recv()
        self.waiting = []

    def second(self):
        self.arrived()
        z, x, y, c = self.p.me
        to = (z, 1 - x, y, c) if self.x_first else (z, x, 1 - y, c)
        self.waiting = [self._copy((ALL, x, y, c), self.p.device(*to), 3)]

    def third(self):
        self.arrived()
        z, x, y, c = self.p.me
        if self.x_first:
            part, to = (ALL, ALL, y, c), (z, x, 1 - y, c)
        else:
            part, to = (ALL, x, ALL, c), (z, 1 - x, y, c)
        self.waiting = [self._copy(part, self.p.device(*to), 4)]

    def sibling(self):
        self.arrived()
        z, x, y, c = self.p.me
        self.waiting = [
            self._copy((ALL, ALL, ALL, c), self.p.device(z, x, y, 1 - c), 5)
        ]

    def close(self):
        for copy in self.started:
            copy.wait_send()
        self.started = []


class Scatter:
    def __init__(self, place, part, bufs, x_last, send, recv):
        self.p, self.part, self.bufs, self.x_last = place, part, bufs, x_last
        self.send, self.recv = send, recv

    def _copy(self, src, dst, device, slot):
        copy = pltpu.make_async_remote_copy(
            src_ref=src,
            dst_ref=dst,
            send_sem=self.send(slot),
            recv_sem=self.recv(slot),
            device_id=device,
            device_id_type=MESH,
        )
        copy.start()
        return copy

    def sibling(self):
        z, x, y, c = self.p.me
        self.started = [
            self._copy(
                self.part(ALL, ALL, ALL, 1 - c),
                self.bufs[0],
                self.p.device(z, x, y, 1 - c),
                5,
            )
        ]

    def add(self, part, buf):
        part[...] = part[...] + buf[...]

    def second(self):
        z, x, y, c = self.p.me
        self.started[-1].wait_recv()
        self.add(self.part(ALL, ALL, ALL, c), self.bufs[0])
        if self.x_last:
            part, to = (ALL, ALL, 1 - y, c), (z, x, 1 - y, c)
        else:
            part, to = (ALL, 1 - x, ALL, c), (z, 1 - x, y, c)
        self.started.append(
            self._copy(self.part(*part), self.bufs[1], self.p.device(*to), 4)
        )

    def third(self):
        z, x, y, c = self.p.me
        self.started[-1].wait_recv()
        part = (ALL, ALL, y, c) if self.x_last else (ALL, x, ALL, c)
        self.add(self.part(*part), self.bufs[1])
        if self.x_last:
            part, to = (ALL, 1 - x, y, c), (z, 1 - x, y, c)
        else:
            part, to = (ALL, x, 1 - y, c), (z, x, 1 - y, c)
        self.started.append(
            self._copy(self.part(*part), self.bufs[2], self.p.device(*to), 3)
        )

    def along_z(self):
        z, x, y, c = self.p.me
        self.started[-1].wait_recv()
        self.add(self.part(ALL, x, y, c), self.bufs[2])
        for i, other in enumerate(self.p.zs):
            self.started.append(
                self._copy(
                    self.part(other, x, y, c),
                    self.bufs[3].at[i],
                    self.p.device(other, x, y, c),
                    i,
                )
            )

    def total(self):
        for copy in self.started[-3:]:
            copy.wait_recv()
        out = self.part(*self.p.me)[...].astype(f32)
        for i in range(3):
            out = out + self.bufs[3][i].astype(f32)
        for copy in self.started:
            copy.wait_send()
        return out


def gather_kernel(
    qkv, out, fc_in, down, small, ag_q, ag_o, ag_i, ag_d, ag_s, own, send, recv
):
    place = Place()
    me = place.me
    units = []
    locals_ = []

    def own_copy(src, dst):
        copy = pltpu.make_async_copy(src, dst, own.at[len(locals_)])
        copy.start()
        locals_.append(copy)
        return copy

    def unit(copies, views):
        n = len(units)
        units.append(
            (
                copies,
                [
                    Gather(
                        place,
                        view,
                        k == 0,
                        lambda s, n=n, k=k: send.at[n, k, s],
                        lambda s, n=n, k=k: recv.at[n, k, s],
                    )
                    for k, view in enumerate(views)
                ],
            )
        )

    def q_unit(g):
        copies = [
            own_copy(
                qkv.at[:, pl.ds(1024 * j + 256 * g, 256)],
                ag_q.at[(g,) + me + (ALL, pl.ds(256 * j, 256))],
            )
            for j in range(3)
        ]
        unit(
            copies,
            [
                lambda *i, h=h: ag_q.at[(g,) + i + (pl.ds(16 * h, 16),)]
                for h in range(2)
            ],
        )

    unit([own_copy(small, ag_s.at[me])], [lambda *i: ag_s.at[i]])
    q_unit(0)
    unit(
        [own_copy(out, ag_o.at[me])],
        [lambda *i, h=h: ag_o.at[i + (pl.ds(16 * h, 16),)] for h in range(2)],
    )
    for g in range(1, QG):
        q_unit(g)
    for j in range(MC):
        unit(
            [
                own_copy(fc_in.at[:, pl.ds(512 * j, 512)], ag_i.at[(j,) + me]),
                own_copy(down.at[pl.ds(16 * j, 16)], ag_d.at[(j,) + me]),
            ],
            [lambda *i, j=j: ag_i.at[(j,) + i], lambda *i, j=j: ag_d.at[(j,) + i]],
        )
    place.greet()
    count = len(units)
    ahead = 2
    for t in range(-ahead, count + 4):
        n = t + ahead
        if n < count:
            for copy in units[n][0]:
                copy.wait()
            for array in units[n][1]:
                array.along_z()
        for lag, step in ((1, "second"), (2, "third"), (3, "sibling"), (4, "arrived")):
            if 0 <= t - lag < count:
                for array in units[t - lag][1]:
                    getattr(array, step)()
    for _, arrays in units:
        for array in arrays:
            array.close()


def scatter_kernel(
    gq, go, gi, gd, gs, out_q, out_o, out_i, out_d, out_s,
    part, r1, r2, r3, rz, part_s, s1, s2, s3, sz, load, send, recv,
):
    place = Place()
    place.greet()
    units = []

    def unit(sources, width, store):
        n = len(units)
        slot = n % 2
        arrays = []
        for k in range(2):
            arrays.append(
                Scatter(
                    place,
                    lambda *i, k=k: part.at[(k, slot) + i + (ALL, pl.ds(0, width))],
                    [
                        b.at[(k, slot) + (ALL,) * d + (ALL, pl.ds(0, width))]
                        for b, d in ((r1, 3), (r2, 2), (r3, 1), (rz, 1))
                    ],
                    k == 0,
                    lambda s, n=n, k=k: send.at[n, k, s],
                    lambda s, n=n, k=k: recv.at[n, k, s],
                )
            )
        units.append((sources, arrays, store))

    def q_store(g):
        def store(totals):
            for h in range(2):
                for j in range(3):
                    out_q[pl.ds(16 * h, 16), pl.ds(1024 * j + 256 * g, 256)] = totals[h][
                        :, 256 * j : 256 * (j + 1)
                    ]

        return store

    def o_store(totals):
        for h in range(2):
            out_o[pl.ds(16 * h, 16), :] = totals[h]

    def m_store(j):
        def store(totals):
            for h in range(2):
                out_i[pl.ds(16 * h, 16), pl.ds(512 * j, 512)] = totals[0][
                    :, 512 * h : 512 * (h + 1)
                ]
            out_d[pl.ds(16 * j, 16), :] = totals[1]

        return store

    for g in range(QG):
        unit([gq.at[g, h] for h in range(2)], 768, q_store(g))
    unit([go.at[h] for h in range(2)], 1024, o_store)
    for j in range(MC):
        unit([gi.at[j], gd.at[j]], 1024, m_store(j))
    count = len(units)

    def begin(n):
        sources, arrays, _ = units[n]
        copies = []
        for k in range(2):
            copy = pltpu.make_async_copy(
                sources[k],
                arrays[k].part(ALL, ALL, ALL, ALL),
                load.at[k],
            )
            copy.start()
            copies.append(copy)
        for k in range(2):
            copies[k].wait()
            arrays[k].sibling()

    def end(n):
        _, arrays, store = units[n]
        store([array.total() for array in arrays])

    for t in range(0, 2 * count + 4):
        for n in range(count):
            step = t - 2 * n
            if step == 4:
                end(n)
        for n in range(count):
            step = t - 2 * n
            if 1 <= step <= 3:
                for array in units[n][1]:
                    (array.second, array.third, array.along_z)[step - 1]()
            if step == 0:
                begin(n)
    tiny = Scatter(
        place,
        lambda *i: part_s.at[i],
        [s1, s2, s3, sz],
        True,
        lambda s: send.at[count, 0, s],
        lambda s: recv.at[count, 0, s],
    )
    copy = pltpu.make_async_copy(gs, part_s, load.at[0])
    copy.start()
    copy.wait()
    tiny.sibling()
    tiny.second()
    tiny.third()
    tiny.along_z()
    out_s[...] = tiny.total()


def gather_all(qkv, out, fc_in, down, small):
    any_ = pl.BlockSpec(memory_space=pl.ANY)
    sd = jax.ShapeDtypeStruct
    ranks = (4, 2, 2, 2)
    return pl.pallas_call(
        gather_kernel,
        out_shape=[
            sd((QG,) + ranks + (32, 768), bf16),
            sd(ranks + (32, 1024), bf16),
            sd((MC,) + ranks + (32, 512), bf16),
            sd((MC,) + ranks + (16, 1024), bf16),
            sd(ranks + (16, 128), bf16),
        ],
        in_specs=[any_] * 5,
        out_specs=[any_] * 5,
        scratch_shapes=[
            pltpu.SemaphoreType.DMA((30,)),
            pltpu.SemaphoreType.DMA((14, 2, 6)),
            pltpu.SemaphoreType.DMA((14, 2, 6)),
        ],
        compiler_params=pltpu.CompilerParams(collective_id=0, has_side_effects=True),
    )(qkv, out, fc_in, down, small)


def scatter_all(gq, go, gi, gd, gs):
    any_ = pl.BlockSpec(memory_space=pl.ANY)
    vmem = pl.BlockSpec(memory_space=pltpu.VMEM)
    sd = jax.ShapeDtypeStruct
    return pl.pallas_call(
        scatter_kernel,
        out_shape=[
            sd((32, 3072), f32),
            sd((32, 1024), f32),
            sd((32, 4096), f32),
            sd((128, 1024), f32),
            sd((8, 128), f32),
        ],
        in_specs=[any_] * 5,
        out_specs=[vmem] * 5,
        scratch_shapes=[
            pltpu.VMEM((2, 2, 4, 2, 2, 2, 16, 1024), bf16),
            pltpu.VMEM((2, 2, 4, 2, 2, 16, 1024), bf16),
            pltpu.VMEM((2, 2, 4, 2, 16, 1024), bf16),
            pltpu.VMEM((2, 2, 4, 16, 1024), bf16),
            pltpu.VMEM((2, 2, 3, 16, 1024), bf16),
            pltpu.VMEM((4, 2, 2, 2, 8, 128), f32),
            pltpu.VMEM((4, 2, 2, 8, 128), f32),
            pltpu.VMEM((4, 2, 8, 128), f32),
            pltpu.VMEM((4, 8, 128), f32),
            pltpu.VMEM((3, 8, 128), f32),
            pltpu.SemaphoreType.DMA((2,)),
            pltpu.SemaphoreType.DMA((14, 2, 6)),
            pltpu.SemaphoreType.DMA((14, 2, 6)),
        ],
        compiler_params=pltpu.CompilerParams(
            collective_id=1, has_side_effects=True, vmem_limit_bytes=40 * 2**20
        ),
    )(gq, go, gi, gd, gs)


def layer_math(
    tokens, cotangent, seq_lens, gain, shift, qkv_matrix, qkv_b, out_matrix, out_b,
    in_matrix, in_b, down_matrix, down_b,
):
    gain_full, shift_full = gain.astype(f32), shift.astype(f32)
    row_count, width = tokens.shape
    inputs = tokens.astype(f32)
    centred = inputs - jnp.mean(inputs, axis=-1, keepdims=True)
    inverse = lax.rsqrt(jnp.mean(centred * centred, axis=-1, keepdims=True) + epsilon)
    normed = centred * inverse
    hid_low = (normed * gain_full + shift_full).astype(bf16)
    qkv = jnp.dot(hid_low, qkv_matrix, preferred_element_type=f32) + qkv_b.astype(f32)
    segment, places, offset = positions(seq_lens[0], row_count)
    freqs = 10000.0 ** (-jnp.arange(ROT // 2, dtype=f32) * 2.0 / ROT)
    angle = offset[:, None] * freqs[None, :]
    cosine = jnp.cos(angle)[:, None, :]
    sine = jnp.sin(angle)[:, None, :]
    heads = (row_count, HEADS, HEAD)
    q_low = rotate(qkv[:, :width].reshape(heads), cosine, sine).astype(bf16)
    k_low = rotate(qkv[:, width : 2 * width].reshape(heads), cosine, sine).astype(bf16)
    v_low = qkv[:, 2 * width :].reshape(heads).astype(bf16)
    block_rows = min(512, row_count)
    block_count = row_count // block_rows
    outputs = []
    kept_lse = []
    for block in range(block_count):
        lower = block * block_rows
        upper = lower + block_rows
        scores, allowed = block_scores(
            q_low[lower:upper], k_low[:upper], segment[lower:upper], segment[:upper],
            places[lower:upper], places[:upper],
        )
        row_max = jnp.max(scores, axis=-1, keepdims=True)
        expo = jnp.exp(scores - row_max)
        totals = jnp.sum(expo, axis=-1, keepdims=True)
        soft_low = (expo / totals).astype(bf16)
        kept_lse.append(row_max + jnp.log(totals))
        outputs.append(
            jnp.einsum("hqk,khd->qhd", soft_low, v_low[:upper], preferred_element_type=f32)
        )
    att_low = jnp.concatenate(outputs, axis=0).reshape(row_count, width).astype(bf16)
    attn_out = jnp.dot(att_low, out_matrix, preferred_element_type=f32) + out_b.astype(f32)
    pre = jnp.dot(hid_low, in_matrix, preferred_element_type=f32) + in_b.astype(f32)
    gelu_exact = partial(jax.nn.gelu, approximate=False)
    act_low = gelu_exact(pre).astype(bf16)
    mlp = jnp.dot(act_low, down_matrix, preferred_element_type=f32) + down_b.astype(f32)
    mixed = (inputs + attn_out + mlp).astype(bf16)
    stream_rms = jnp.sqrt(
        jnp.stack([jnp.mean(inputs * inputs), jnp.mean(attn_out * attn_out), jnp.mean(mlp * mlp)])
    )[None, :]
    upstream = cotangent.astype(f32)
    grad_down = transposed_times(act_low, cotangent)
    grad_out = transposed_times(att_low, cotangent)
    grad_sum = jnp.sum(upstream, axis=0)
    act_grad = times_transposed(cotangent, down_matrix)
    _, gelu_pull = jax.vjp(gelu_exact, pre)
    pre_grad_low = gelu_pull(act_grad)[0].astype(bf16)
    grad_in = transposed_times(hid_low, pre_grad_low)
    grad_in_b = jnp.sum(pre_grad_low.astype(f32), axis=0)
    att_grad_low = times_transposed(cotangent, out_matrix).astype(bf16).reshape(heads)
    query_grads = []
    key_grad = jnp.zeros(heads, f32)
    value_grad = jnp.zeros(heads, f32)
    for block in range(block_count):
        lower = block * block_rows
        upper = lower + block_rows
        query_block = q_low[lower:upper]
        scores, allowed = block_scores(
            query_block, k_low[:upper], segment[lower:upper], segment[:upper],
            places[lower:upper], places[:upper],
        )
        soft = jnp.where(allowed[None], jnp.exp(scores - kept_lse[block]), 0.0)
        soft_low = soft.astype(bf16)
        out_grad = att_grad_low[lower:upper]
        value_part = jnp.einsum("hqk,qhd->khd", soft_low, out_grad, preferred_element_type=f32)
        prob_grad = jnp.einsum("qhd,khd->hqk", out_grad, v_low[:upper], preferred_element_type=f32)
        score_grad = soft * (prob_grad - jnp.sum(soft * prob_grad, axis=-1, keepdims=True))
        score_low = score_grad.astype(bf16)
        query_grads.append(
            jnp.einsum("hqk,khd->qhd", score_low, k_low[:upper], preferred_element_type=f32)
            * HEAD ** (-0.5)
        )
        key_part = jnp.einsum(
            "hqk,qhd->khd", score_low, query_block, preferred_element_type=f32
        ) * HEAD ** (-0.5)
        padding = ((0, row_count - upper), (0, 0), (0, 0))
        key_grad = key_grad + jnp.pad(key_part, padding)
        value_grad = value_grad + jnp.pad(value_part, padding)
    query_grad = unrotate(jnp.concatenate(query_grads, axis=0), cosine, sine)
    key_grad = unrotate(key_grad, cosine, sine)
    qkv_grad_low = jnp.concatenate(
        [g.reshape(row_count, width) for g in (query_grad, key_grad, value_grad)], axis=1
    ).astype(bf16)
    grad_qkv = transposed_times(hid_low, qkv_grad_low)
    grad_qkv_b = jnp.sum(qkv_grad_low.astype(f32), axis=0)
    hidden_grad = times_transposed(qkv_grad_low, qkv_matrix) + times_transposed(
        pre_grad_low, in_matrix
    )
    grad_gain = jnp.sum(hidden_grad * normed, axis=0)
    grad_shift = jnp.sum(hidden_grad, axis=0)
    scaled = hidden_grad * gain_full
    input_grad = upstream + inverse * (
        scaled
        - jnp.mean(scaled, axis=-1, keepdims=True)
        - normed * jnp.mean(scaled * normed, axis=-1, keepdims=True)
    )
    return (
        mixed, input_grad.astype(bf16), grad_gain, grad_shift, grad_qkv, grad_qkv_b,
        grad_out, grad_sum, grad_in, grad_in_b, grad_down, grad_sum, stream_rms,
    )


def generic(tokens, cotangent, seq_lens, *shards):
    axes = ("wide", "narrow")
    whole = [lax.all_gather(s, axes, axis=0, tiled=True) for s in shards]
    results = layer_math(tokens, cotangent, seq_lens, *whole)
    summed = [
        lax.psum_scatter(g, axes, scatter_dimension=0, tiled=True) for g in results[2:12]
    ]
    return (*results[:2], *summed, results[12])


def local(
    tokens, cotangent, seq_lens, norm_gain, norm_bias, qkv_weight, qkv_bias, out_weight,
    out_bias, fc_in_weight, fc_in_bias, fc_out_weight, fc_out_bias,
):
    in_mixed = fc_in_weight.reshape(32, 32, MC, 16).transpose(0, 2, 1, 3).reshape(32, 4096)
    row0 = jnp.concatenate([norm_gain, norm_bias, out_bias, fc_out_bias])
    small = jnp.zeros((16, 128), bf16)
    small = small.at[0].set(row0).at[1, :96].set(qkv_bias).at[2].set(fc_in_bias)
    ag_q, ag_o, ag_i, ag_d, ag_s = gather_all(
        qkv_weight, out_weight, in_mixed, fc_out_weight, small
    )
    ag_s = ag_s.reshape(32, 16, 128)
    gain, shift, out_b, down_b = (
        ag_s[:, 0, 32 * i : 32 * (i + 1)].reshape(1024) for i in range(4)
    )
    qkv_b = ag_s[:, 1, :96].reshape(3072)
    in_b = ag_s[:, 2].reshape(32, MC, 16).transpose(1, 0, 2).reshape(4096)
    qkv_matrix = (
        ag_q.reshape(QG, 1024, 3, 256).transpose(1, 2, 0, 3).reshape(1024, 3072)
    )
    out_matrix = ag_o.reshape(1024, 1024)
    in_matrix = ag_i.reshape(MC, 1024, 512).transpose(1, 0, 2).reshape(1024, 4096)
    down_matrix = ag_d.reshape(4096, 1024)
    (
        mixed, tokens_grad, g_gain, g_shift, g_qkv, g_qkv_b, g_out, g_sum, g_in, g_in_b,
        g_down, _, stream_rms,
    ) = layer_math(
        tokens, cotangent, seq_lens, gain, shift, qkv_matrix, qkv_b, out_matrix, out_b,
        in_matrix, in_b, down_matrix, down_b,
    )
    ranks = (4, 2, 2, 2)
    gq = (
        g_qkv.astype(bf16)
        .reshape(32, 2, 16, 3, QG, 256)
        .transpose(4, 1, 0, 2, 3, 5)
        .reshape((QG, 2) + ranks + (16, 768))
    )
    go = g_out.astype(bf16).reshape(32, 2, 16, 1024).transpose(1, 0, 2, 3)
    go = go.reshape((2,) + ranks + (16, 1024))
    gi = g_in.astype(bf16).reshape(32, 2, 16, MC, 512).transpose(3, 0, 2, 1, 4)
    gi = gi.reshape((MC,) + ranks + (16, 1024))
    gd = g_down.astype(bf16).reshape((MC,) + ranks + (16, 1024))
    rows = [
        jnp.concatenate([g.reshape(32, 32) for g in (g_gain, g_shift, g_sum, g_sum)], axis=1),
        jnp.pad(g_qkv_b.reshape(32, 96), ((0, 0), (0, 32))),
        g_in_b.reshape(MC, 32, 16).transpose(1, 0, 2).reshape(32, 128),
    ]
    gs = jnp.pad(jnp.stack(rows, axis=1), ((0, 0), (0, 5), (0, 0)))
    out_q, out_o, out_i, out_d, out_s = scatter_all(
        gq, go, gi, gd, gs.reshape(ranks + (8, 128))
    )
    out_i = out_i.reshape(32, MC, 32, 16).transpose(0, 2, 1, 3).reshape(32, 4096)
    return (
        mixed, tokens_grad, out_s[0, :32], out_s[0, 32:64], out_q, out_s[1, :96], out_o,
        out_s[0, 64:96], out_i, out_s[2], out_d, out_s[0, 96:], stream_rms,
    )


def solution(mesh):
    rows, flat = P(("wide", "narrow"), None), P(("wide", "narrow"))
    fits = mesh.shape["wide"] == 8 and mesh.shape["narrow"] == 4
    return jax.shard_map(
        local if fits else generic,
        mesh=mesh,
        in_specs=(rows, rows, rows, flat, flat, rows, flat, rows, flat, rows, flat, rows, flat),
        out_specs=(rows, rows, flat, flat, rows, flat, rows, flat, rows, flat, rows, flat, rows),
        check_vma=False,
    )
```

time: 988 us -> 903 us (0.914)
  waiting for transfers between devices: 375 us -> 0 us
  Pallas kernels: 0 us -> 292 us
  local copies, waits for them, and re-layouts: 48.8 us -> 190 us
  blocking collectives: 125 us -> 0 us
  between operations: 17 us -> 3.98 us
    reduce_scatter x4 -> x0, waiting for transfers between devices: 342 us -> none  [the longest x1 187 us: local(): lax.psum_scatter(grad_in_matrix, ('wide', 'narrow'), scatter_dimension=0,...]
    pallas_call x0 -> x2, Pallas kernels: none -> 292 us  [the longest x1 166 us: scatter_all(): pl.pallas_call(scatter_kernel, out_shape=[sd((32, 3072), f32), sd((32, 10...]
    reshape x0 -> x14, local copies, waits for them, and re-layouts: none -> 103 us  [the longest x3 40.9 us: local(): gq = g_qkv.astype(bf16).reshape(32, 2, 16, 3, QG, 256).transpose(4, 1, 0,...]
    unnamed x2 -> x0, blocking collectives: 84.4 us -> none
    all_gather x1 -> x0, blocking collectives: 40.7 us -> none  [local(): lax.all_gather(shards[7], ('wide', 'narrow'), axis=0, tiled=True)]
    dot_general x14, matrix products: 166 us -> 204 us  [the longest x1 51.4 us: layer_math(): jnp.dot(hid_low, in_matrix, preferred_element_type=f32) + in_b.astype(f32)]
    dot_general x4, matrix products: 83.5 us -> 50.2 us  [times_transposed(): lax.dot_general(left, right, (((1,), (1,)), ((), ())), preferred_element_...]
    all_gather x4 -> x0, waiting for transfers between devices: 30.5 us -> none  [the longest x1 30.5 us: local(): lax.all_gather(shards[2], ('wide', 'narrow'), axis=0, tiled=True)]
  transfers between devices with their start and end apart: 8 -> 0, of which waited for: 3 -> 0; matrix products, arithmetic and copies ran while one was open for 46% -> 0% of each run, Pallas kernels for 0% -> 0%
where the time goes in v1:
time: 903 us; the launch traced here: 893 us
  matrix products  321 us (36%)
  Pallas kernels  292 us (32%)
  local copies, waits for them, and re-layouts  190 us (21%)
  other arithmetic  86.6 us (10%)
    pallas_call x1, Pallas kernels, scatter_all(): pl.pallas_call(scatter_kernel, out_shape=[sd((32, 3072), f32), sd((32, 10...  166 us
    pallas_call x1, Pallas kernels, gather_all(): pl.pallas_call(gather_kernel, out_shape=[sd((QG,) + ranks + (32, 768), bf...  126 us
    dot_general x1, matrix products, layer_math(): jnp.dot(hid_low, in_matrix, preferred_element_type=f32) + in_b.astype(f32)  51.4 us
    dot_general x4, matrix products, times_transposed(): lax.dot_general(left, right, (((1,), (1,)), ((), ())), preferred_element_...  50.2 us
    dot_general x4, matrix products, transposed_times(): lax.dot_general(left, right, (((0,), (0,)), ((), ())), preferred_element_...  46 us
    reshape x3, local copies, waits for them, and re-layouts, local(): gq = g_qkv.astype(bf16).reshape(32, 2, 16, 3, QG, 256).transpose(4, 1, 0,...  40.9 us
    convert_element_type x2, other arithmetic, layer_math(): score_low = score_grad.astype(bf16)  40.4 us
    dot_general x2, matrix products, layer_math(): jnp.einsum('qhd,khd->hqk', out_grad, v_low[:upper], preferred_element_typ...  39.4 us

profile of v1, /device:TPU:0, one launch (start us, length us, event | category | flops | bytes accessed | tf_op | source)
XLA Modules:
  0.0 893.3 jit_solution(17412781203814264631)
XLA Ops:
  13.3 126.2 %shard_map.228 = (bf16[4,4,2,2,2,32,768]{6,5,4,3,2,1,0:T(8,128)(2,1)}, bf16[4,2,2,2,32,1024]{5,4,3,2,1,0:T(8,128)(2,1)}, bf16[8,4,2,2,2,32,512]{6,5,4,3,2,1,0:T(...) custom-call(bf16[32,3072]{1,0:T(8,128)(2,1)} %qkv.1, bf16[32,1024]{1,0:T(8,128)(2,1)} %out.1, ...), custom_call_target="tpu_custom_call" | custom-call | tf_op jit(solution)/shard_map/pallas_call | solution.py:435
  151.1 17.8 %reshape.521 = bf16[4,1024,3,256]{3,2,1,0:T(4,128)(2,1)} reshape(bf16[4,4,2,2,2,32,768]{6,5,4,3,2,1,0:T(8,128)(2,1)} %get-tuple-element.60) | data formatting | bytes 12582912 | tf_op jit(solution)/shard_map/reshape | solution.py:631
  168.9 13.0 %copy.95 = bf16[1024,3,4,256]{0,3,2,1:T(8,128)(2,1)} copy(bf16[1024,3,4,256]{3,1,0,2:T(4,128)(2,1)} %bitcast.153) | data formatting | bytes 12582912 | tf_op jit(solution)/shard_map/transpose | solution.py:631
  271.0 12.9 %multiply_reduce_fusion.1 = (f32[16,512]{1,0:T(8,128)S(1)}, f32[16,512,512]{1,2,0:T(8,128)}) fusion(f32[16,512]{1,0:T(8,128)} %log_add_fusion.1, f32[16,512,512]{1,2,0:T(8,128)} %get-tuple-element.153, pred[512,512]{0,1:T(8,128)(4,1)} %copy-done.21, bf16[512,16,64]{0,2,1:T(8,128)(2,1)} %bitcast.196, bf16[512,16,64]{0,2,1:T(8,128)(2,1)} %bitcast.188), kind=kOutput, calls=%fused_computation.23 | convolution fusion | flops 562028544 | bytes 35979264 | tf_op jit(solution)/shard_map/qhd,khd->hqk/dot_general | solution.py:566
  284.0 12.6 %multiply_convert_fusion.1 = bf16[16,512,512]{1,2,0:T(8,128)(2,1)S(1)} fusion(f32[16,512,512]{1,2,0:T(8,128)} %get-tuple-element.156, f32[16,512]{1,0:T(8,128)S(1)} %get-tuple-element.155, f32[16,512]{1,0:T(8,128)S(1)} %copy-done.35, f32[16,512,512]{1,2,0:T(8,128)} %get-tuple-element.153, pred[512,512]{0,1:T(8,128)(4,1)S(1)} %copy-done.22), kind=kLoop, calls=%fused_computation.22 | loop fusion | flops 29360128 | bytes 42270720 | tf_op jit(solution)/shard_map/convert_element_type | solution.py:568
  303.4 13.8 %fusion.1 = (f32[16,512]{1,0:T(8,128)S(1)}, f32[16,512,1024]{2,1,0:T(8,128)}) fusion(pred[512,1024]{1,0:T(8,128)(4,1)S(1)} %fusion.48, bf16[1024,16,48]{0,2,1:T(8,128)(2,1)S(1)} %copy-done.7, bf16[1024,16,8]{0,2,1:T(8,128)(2,1)S(1)} %get-tuple-element.126, bf16[1024,16,8]{0,2,1:T(8,128)(2,1)S(1)} %get-tuple-element.125, bf16[1024,16,64]{0,2,1:T(8,128)(2,1)S(1)} %copy-done.9), kind=kOutput, calls=%fused_computation.8 | convolution fusion | flops 1105190912 | bytes 37257216 | tf_op jit(solution)/shard_map/qhd,khd->hqk/dot_general | solution.py:62
  317.2 14.9 %fusion = f32[16,512]{1,0:T(8,128)S(1)} fusion(f32[16,512,1024]{2,1,0:T(8,128)} %get-tuple-element.151, f32[16,512]{1,0:T(8,128)S(1)} %get-tuple-element.150, pred[512,1024]{1,0:T(8,128)(4,1)S(1)} %fusion.48), kind=kLoop, calls=%fused_computation.6 | loop fusion | flops 33546240 | bytes 34144256 | tf_op jit(solution)/shard_map/reduce_sum | solution.py:525
  332.2 17.8 %fusion.40 = bf16[1024,16,64]{0,2,1:T(8,128)(2,1)} fusion(f32[512,16,64]{0,2,1:T(8,128)} %fusion.49, bf16[512,16,64]{0,2,1:T(8,128)(2,1)} %bitcast.193, f32[16,512]{1,0:T(8,128)S(1)} %log_add_fusion, f32[16,512,1024]{2,1,0:T(8,128)} %get-tuple-element.151, pred[512,1024]{1,0:T(8,128)(4,1)S(1)} %fusion.48), kind=kOutput, calls=%fused_computation.84 | convolution fusion | flops 1117782016 | bytes 39354368 | tf_op jit(solution)/shard_map/hqk,qhd->khd/dot_general | solution.py:565
  350.0 14.8 %fusion.53 = bf16[16,64,512]{2,1,0:T(8,128)(2,1)S(1)} fusion(bf16[1024,16,64]{0,2,1:T(8,128)(2,1)S(1)} %bitcast.180, f32[16,512,1024]{2,1,0:T(8,128)} %get-tuple-element.151, f32[16,512]{1,0:T(8,128)S(1)} %fusion, f32[16,512]{1,0:T(8,128)S(1)} %get-tuple-element.150, pred[512,1024]{1,0:T(8,128)(4,1)S(1)} %fusion.48), kind=kOutput, calls=%fused_computation.113 | convolution fusion | flops 1116209152 | bytes 37289984 | tf_op jit(solution)/shard_map/hqk,khd->qhd/dot_general | solution.py:529
  367.7 26.5 %multiply_reduce_fusion = (f32[16,512]{1,0:T(8,128)S(1)}, f32[16,512,1024]{2,1,0:T(8,128)}) fusion(f32[16,512]{1,0:T(8,128)S(1)} %log_add_fusion, f32[16,512,1024]{2,1,0:T(8,128)} %get-tuple-element.151, pred[512,1024]{1,0:T(8,128)(4,1)S(1)} %fusion.48, bf16[512,16,64]{0,2,1:T(8,128)(2,1)S(1)} %bitcast.194, bf16[1024,16,64]{0,2,1:T(8,128)(2,1)S(1)} %bitcast.181), kind=kOutput, calls=%fused_computation.1 | convolution fusion | flops 1124065280 | bytes 70844416 | tf_op jit(solution)/shard_map/qhd,khd->hqk/dot_general | solution.py:566
  394.2 27.8 %multiply_convert_fusion = bf16[16,512,1024]{2,1,0:T(8,128)(2,1)} fusion(f32[16,512,1024]{2,1,0:T(8,128)} %get-tuple-element.158, f32[16,512]{1,0:T(8,128)S(1)} %get-tuple-element.157, f32[16,512]{1,0:T(8,128)S(1)} %log_add_fusion, f32[16,512,1024]{2,1,0:T(8,128)} %get-tuple-element.151, pred[512,1024]{1,0:T(8,128)(4,1)S(1)} %fusion.48), kind=kLoop, calls=%fused_computation | loop fusion | flops 58720256 | bytes 84475904 | tf_op jit(solution)/shard_map/convert_element_type | solution.py:568
  433.7 12.8 %multiply_bitcast_fusion.1 = f32[512,16,64]{0,2,1:T(8,128)} fusion(bf16[16,512,1024]{2,1,0:T(8,128)(2,1)} %multiply_convert_fusion, bf16[1024,16,48]{0,2,1:T(8,128)(2,1)} %copy-done.6, bf16[1024,16,8]{0,2,1:T(8,128)(2,1)S(1)} %copy-done.20, bf16[1024,16,8]{0,2,1:T(8,128)(2,1)S(1)} %copy-done.18), kind=kOutput, calls=%fused_computation.104 | convolution fusion | flops 1080557568 | bytes 20971520 | tf_op jit(solution)/shard_map/hqk,khd->qhd/dot_general | solution.py:570
  469.3 12.9 %convolution_convert_fusion.2 = bf16[1024,3072]{1,0:T(8,128)(2,1)} fusion(bf16[1024,1024]{0,1:T(8,128)(2,1)} %bitcast.182, bf16[1024,1024]{0,1:T(8,128)(2,1)} %bitcast.173, bf16[1024,1024]{0,1:T(8,128)(2,1)} %bitcast.170, bf16[1024,1024]{1,0:T(8,128)(2,1)S(1)} %copy-done.12, f32[1024]{0:T(1024)S(1)} %copy-done.46, f32[1024]{0:T(1024)S(1)} %copy-done.44, ...), kind=kOutput, calls=%fused_computation.59 | convolution fusion | flops 6470762496 | bytes 14696448 | tf_op jit(solution)/shard_map/dot_general | solution.py:56
  505.9 17.8 %reshape.535.gq = bf16[4,2,4,2,2,2,16,768]{7,6,5,4,3,2,1,0:T(8,128)(2,1)} reshape(bf16[4,2,32,16,3,256]{5,4,3,2,1,0:T(4,128)(2,1)} %bitcast.154) | data formatting | bytes 12582912 | tf_op jit(solution)/shard_map/reshape | solution.py:648
  523.7 51.4 %multiply_convert_fusion.2 = (bf16[1024,4096]{1,0:T(8,128)(2,1)}, f32[1024,4096]{1,0:T(8,128)}, f32[1024,4096]{1,0:T(8,128)}) fusion(f32[4096]{0:T(1024)S(1)} %copy-done.42, bf16[1024,4096]{0,1:T(8,128)(2,1)} %bitcast.164, bf16[1024,1024]{1,0:T(8,128)(2,1)} %param.19, f32[1024]{0:T(1024)S(1)} %copy-done.46, f32[1024]{0:T(1024)S(1)} %copy-done.44, ...), kind=kOutput, calls=%fused_computation.25 | convolution fusion | flops 8873050112 | bytes 52461568 | tf_op jit(solution)/shard_map/dot_general | solution.py:533
  575.2 23.6 %convert_reduce_fusion = (f32[4096]{0:T(1024)S(1)}, bf16[1024,4096]{1,0:T(8,128)(2,1)}) fusion(f32[1024,4096]{1,0:T(8,128)} %get-tuple-element.118, bf16[4096,1024]{1,0:T(8,128)(2,1)} %bitcast.206, bf16[1024,1024]{1,0:T(8,128)(2,1)S(1)} %copy-done.52, f32[1024,4096]{1,0:T(8,128)} %get-tuple-element.154, f32[4096]{0:T(1024)S(1)} %copy-done.42), kind=kOutput, calls=%fused_computation.19 | convolution fusion | flops 8661233664 | bytes 52461568 | tf_op jit(solution)/shard_map/dot_general | solution.py:50
  598.7 15.2 %fusion.92 = f32[1024,1024]{1,0:T(8,128)} fusion(bf16[1024,4096]{1,0:T(8,128)(2,1)} %get-tuple-element.117, bf16[4096,1024]{1,0:T(8,128)(2,1)} %bitcast.207), kind=kOutput, calls=%fused_computation.189 | convolution fusion | flops 8589934592 | bytes 20971520 | tf_op jit(solution)/shard_map/dot_general | solution.py:536
  613.9 13.8 %fusion.34 = (f32[1024]{0:T(1024)S(1)}, f32[1024]{0:T(1024)S(1)}, f32[1024]{0:T(1024)S(1)}, f32[1024]{0:T(1024)S(1)}, f32[]{:T(128)}, /*index=5*/f32[1024,1024]{1,0:T(8,128)}) fusion(bf16[1024,1024]{1,0:T(8,128)(2,1)S(1)} %copy-done.13, f32[1024]{0:T(1024)S(1)} %copy-done.50, f32[1024]{0:T(1024)S(1)} %copy-done.41, f32[1024]{0:T(1024)S(1)} %copy-done.44, ...), kind=kOutput, calls=%fused_computation.77 | convolution fusion | flops 8603561984 | bytes 27291652 | tf_op jit(solution)/shard_map/dot_general | solution.py:50
  628.5 15.3 %convolution_convert_fusion = bf16[4096,1024]{1,0:T(8,128)(2,1)} fusion(bf16[1024,4096]{1,0:T(8,128)(2,1)} %get-tuple-element.117, bf16[1024,1024]{1,0:T(8,128)(2,1)} %param.20), kind=kOutput, calls=%fused_computation.51 | convolution fusion | flops 8594128896 | bytes 18874368 | tf_op jit(solution)/shard_map/dot_general | solution.py:56
  652.2 15.5 %convolution_convert_fusion.1 = bf16[1024,4096]{1,0:T(8,128)(2,1)} fusion(bf16[1024,4096]{1,0:T(8,128)(2,1)} %get-tuple-element.161, bf16[1024,1024]{1,0:T(8,128)(2,1)} %param.19, f32[1024]{0:T(1024)S(1)} %copy-done.46, f32[1024]{0:T(1024)S(1)} %copy-done.44, f32[1024]{0:T(1024)S(1)} %copy-done.50, f32[1024]{0:T(1024)S(1)} %copy-done.41), kind=kOutput, calls=%fused_computation.52 | convolution fusion | flops 8600420352 | bytes 18890752 | tf_op jit(solution)/shard_map/dot_general | solution.py:56
  668.2 12.2 %copy.122 = bf16[128,8,8,512]{3,2,1,0:T(8,128)(2,1)} copy(bf16[128,8,8,512]{3,1,2,0:T(8,128)(2,1)} %bitcast.167) | data formatting | bytes 16777216
  680.4 16.3 %copy.125 = bf16[32,2,16,8,512]{4,1,2,0,3:T(2,128)(2,1)} copy(bf16[32,2,16,8,512]{4,3,2,1,0:T(8,128)(2,1)} %bitcast.155) | data formatting | bytes 16777216 | tf_op jit(solution)/shard_map/reshape | solution.py:652
  696.7 14.4 %reshape.539.gi = bf16[8,4,2,2,2,16,1024]{6,5,4,3,2,1,0:T(8,128)(2,1)} reshape(bf16[8,32,16,2,512]{4,3,2,1,0:T(2,128)(2,1)} %bitcast.156) | data formatting | bytes 16777216 | tf_op jit(solution)/shard_map/reshape | solution.py:653
  714.5 165.8 %shard_map.229 = (f32[32,3072]{1,0:T(8,128)S(1)}, f32[32,1024]{1,0:T(8,128)S(1)}, f32[32,4096]{1,0:T(8,128)S(1)}, f32[128,1024]{1,0:T(8,128)S(1)}, f32[8,128]{1,0:T(8,128)S(1)}) custom-call(bf16[4,2,4,2,2,2,16,768]{7,6,5,4,3,2,1,0:T(8,128)(2,1)S(1)} %copy-done, bf16[2,4,2,2,2,16,1024]{6,5,4,3,2,1,0:T(8,128)(2,1)S(1)} %bitcast.151, ...), custom_call_target="tpu_custom_call" | custom-call | tf_op jit(solution)/shard_map/pallas_call | solution.py:459
  (218 shorter events, 204.4 us)
Async XLA Ops:
  6.5 186.9 %copy-start.40 = (f32[1024]{0:T(1024)}, f32[1024]{0:T(1024)S(1)}, u32[]{:S(2)}) copy-start(f32[1024]{0:T(1024)S(1)} %broadcast_multiply_fusion.2) | copy-start | bytes 12292
  8.8 184.6 %copy-start.49 = (f32[1024]{0:T(1024)}, f32[1024]{0:T(1024)S(1)}, u32[]{:S(2)}) copy-start(f32[1024]{0:T(1024)S(1)} %add_rsqrt_fusion) | copy-start | bytes 12292
  10.0 232.7 %copy-start.21 = (pred[512,512]{0,1:T(8,128)(4,1)}, pred[512,512]{0,1:T(8,128)(4,1)S(1)}, u32[]{:S(2)}) copy-start(pred[512,512]{0,1:T(8,128)(4,1)S(1)} %compare_and_fusion) | copy-start | bytes 786436
  143.3 50.1 %copy-start.43 = (f32[1024]{0:T(1024)}, f32[1024]{0:T(1024)S(1)}, u32[]{:S(2)}) copy-start(f32[1024]{0:T(1024)S(1)} %reshape.549) | copy-start | bytes 12292
  143.4 50.1 %copy-start.45 = (f32[1024]{0:T(1024)}, f32[1024]{0:T(1024)S(1)}, u32[]{:S(2)}) copy-start(f32[1024]{0:T(1024)S(1)} %reshape.550) | copy-start | bytes 12292
  232.6 70.8 %copy-start.17 = (bf16[1024,16,8]{0,2,1:T(8,128)(2,1)}, bf16[1024,16,8]{0,2,1:T(8,128)(2,1)S(1)}, u32[]{:S(2)}) copy-start(bf16[1024,16,8]{0,2,1:T(8,128)(2,1)S(1)} %get-tuple-element.125) | copy-start | bytes 786436
  232.6 70.8 %copy-start.19 = (bf16[1024,16,8]{0,2,1:T(8,128)(2,1)}, bf16[1024,16,8]{0,2,1:T(8,128)(2,1)S(1)}, u32[]{:S(2)}) copy-start(bf16[1024,16,8]{0,2,1:T(8,128)(2,1)S(1)} %get-tuple-element.126) | copy-start | bytes 786436
  332.1 17.8 %copy-start.23 = (bf16[1024,1024]{0,1:T(8,128)(2,1)S(1)}, bf16[1024,1024]{0,1:T(8,128)(2,1)}, u32[]{:S(2)}) copy-start(bf16[1024,1024]{0,1:T(8,128)(2,1)} %copy.100) | copy-start | bytes 6291460
  349.9 15.1 %copy-start.51 = (bf16[1024,1024]{1,0:T(8,128)(2,1)S(1)}, bf16[1024,1024]{1,0:T(8,128)(2,1)}, u32[]{:S(2)}) copy-start(bf16[1024,1024]{1,0:T(8,128)(2,1)} %param.20) | copy-start | bytes 6291460
  505.9 17.8 %copy-start.42 = (f32[4096]{0:T(1024)S(1)}, f32[4096]{0:T(1024)}, u32[]{:S(2)}) copy-start(f32[4096]{0:T(1024)} %reshape.553) | copy-start | bytes 49156
  523.7 51.4 %copy-start.52 = (bf16[1024,1024]{1,0:T(8,128)(2,1)S(1)}, bf16[1024,1024]{1,0:T(8,128)(2,1)}, u32[]{:S(2)}) copy-start(bf16[1024,1024]{1,0:T(8,128)(2,1)} %param.20) | copy-start | bytes 6291460
  598.7 15.2 %copy-start.10 = (bf16[8,1024,512]{1,2,0:T(8,128)(2,1)S(1)}, bf16[8,1024,512]{1,2,0:T(8,128)(2,1)}, u32[]{:S(2)}) copy-start(bf16[8,1024,512]{1,2,0:T(8,128)(2,1)} %copy.101) | copy-start | bytes 25165828
  598.7 15.2 %copy-start.13 = (bf16[1024,1024]{1,0:T(8,128)(2,1)S(1)}, bf16[1024,1024]{1,0:T(8,128)(2,1)}, u32[]{:S(2)}) copy-start(bf16[1024,1024]{1,0:T(8,128)(2,1)} %param.19) | copy-start | bytes 6291460
  598.7 15.2 %copy-start.57 = (bf16[1024,4096]{1,0:T(8,128)(2,1)S(1)}, bf16[1024,4096]{1,0:T(8,128)(2,1)}, u32[]{:S(2)}) copy-start(bf16[1024,4096]{1,0:T(8,128)(2,1)} %get-tuple-element.161) | copy-start | bytes 25165828
  628.4 15.4 %copy-start.14 = (bf16[1024,1024]{1,0:T(8,128)(2,1)S(1)}, bf16[1024,1024]{1,0:T(8,128)(2,1)}, u32[]{:S(2)}) copy-start(bf16[1024,1024]{1,0:T(8,128)(2,1)} %param.19) | copy-start | bytes 6291460
  628.4 15.4 %copy-start.27 = (bf16[16,64,512]{2,1,0:T(8,128)(2,1)S(1)}, bf16[16,64,512]{2,1,0:T(8,128)(2,1)}, u32[]{:S(2)}) copy-start(bf16[16,64,512]{2,1,0:T(8,128)(2,1)} %fusion.52) | copy-start | bytes 3145732
  628.4 15.4 %copy-start.29 = (bf16[16,64,512]{2,1,0:T(8,128)(2,1)S(1)}, bf16[16,64,512]{2,1,0:T(8,128)(2,1)}, u32[]{:S(2)}) copy-start(bf16[16,64,512]{2,1,0:T(8,128)(2,1)} %copy-done.28) | copy-start | bytes 3145732
  628.4 15.4 %copy-start.47 = (f32[1024]{0:T(1024)S(1)}, f32[1024]{0:T(1024)}, u32[]{:S(2)}) copy-start(f32[1024]{0:T(1024)} %reshape.552) | copy-start | bytes 12292
  628.4 15.4 %copy-start.48 = (f32[1024]{0:T(1024)S(1)}, f32[1024]{0:T(1024)}, u32[]{:S(2)}) copy-start(f32[1024]{0:T(1024)} %reshape.554) | copy-start | bytes 12292
  628.5 15.4 %copy-start.53 = (bf16[1024,1024]{1,0:T(8,128)(2,1)S(1)}, bf16[1024,1024]{1,0:T(8,128)(2,1)}, u32[]{:S(2)}) copy-start(bf16[1024,1024]{1,0:T(8,128)(2,1)} %param.20) | copy-start | bytes 6291460
  628.5 15.4 %copy-start.54 = (bf16[4,2,2,2,32,1024]{5,4,3,2,1,0:T(8,128)(2,1)S(1)}, bf16[4,2,2,2,32,1024]{5,4,3,2,1,0:T(8,128)(2,1)}, u32[]{:S(2)}) copy-start(bf16[4,2,2,2,32,1024]{5,4,3,2,1,0:T(8,128)(2,1)} %get-tuple-element.61) | copy-start | bytes 6291460
  628.5 15.4 %copy-start.55 = (f32[1024,1024]{1,0:T(8,128)S(1)}, f32[1024,1024]{1,0:T(8,128)}, u32[]{:S(2)}) copy-start(f32[1024,1024]{1,0:T(8,128)} %fusion.92) | copy-start | bytes 12582916
  628.5 15.4 %copy-start.56 = (f32[1024,1024]{1,0:T(8,128)S(1)}, f32[1024,1024]{1,0:T(8,128)}, u32[]{:S(2)}) copy-start(f32[1024,1024]{1,0:T(8,128)} %get-tuple-element.159) | copy-start | bytes 12582916
  696.7 14.9 %copy-start.38 = (f32[32,1,128]{2,0,1:T(8,128)S(1)}, f32[32,1,128]{2,0,1:T(8,128)}, u32[]{:S(2)}) copy-start(f32[32,1,128]{2,0,1:T(8,128)} %pad_bitcast_fusion) | copy-start | bytes 49156
  (36 other events, 273.2 us)

commit v2 on v0

v2 whole, which is shorter than its diff:
```python
from functools import partial

import jax
import jax.numpy as jnp
from jax import lax
from jax.experimental import pallas as pl
from jax.experimental.pallas import tpu as pltpu
from jax.sharding import PartitionSpec as P

HEADS = 16
HEAD = 64
ROT = 16
MESH = pl.DeviceIdType.MESH
bf16 = jnp.bfloat16
f32 = jnp.float32
ALL = slice(None)

epsilon = 1e-05


def positions(lengths, count):
    ends = jnp.cumsum(lengths)
    places = jnp.arange(count, dtype=jnp.int32)
    segment = jnp.sum((places[:, None] >= ends[None, :]).astype(jnp.int32), axis=1)
    starts = ends - lengths
    slots = jnp.arange(lengths.shape[0], dtype=jnp.int32)
    begin = jnp.sum(jnp.where(segment[:, None] == slots[None, :], starts[None, :], 0), axis=1)
    return (segment, places, (places - begin).astype(jnp.float32))


def rotate(vector, cosine, sine):
    half = ROT // 2
    first = vector[..., :half]
    second = vector[..., half:ROT]
    return jnp.concatenate(
        [first * cosine - second * sine, second * cosine + first * sine, vector[..., ROT:]], axis=-1
    )


def unrotate(grad, cosine, sine):
    half = ROT // 2
    first = grad[..., :half]
    second = grad[..., half:ROT]
    return jnp.concatenate(
        [first * cosine + second * sine, second * cosine - first * sine, grad[..., ROT:]], axis=-1
    )


def times_transposed(left, right):
    return lax.dot_general(
        left, right, (((1,), (1,)), ((), ())), preferred_element_type=jnp.float32
    )


def transposed_times(left, right):
    return lax.dot_general(
        left, right, (((0,), (0,)), ((), ())), preferred_element_type=jnp.float32
    )


def block_scores(query_block, key_low, seg_query, seg_key, place_query, place_key):
    raw = jnp.einsum(
        "qhd,khd->hqk", query_block, key_low, preferred_element_type=jnp.float32
    ) * HEAD ** (-0.5)
    allowed = (seg_query[:, None] == seg_key[None, :]) & (
        place_key[None, :] <= place_query[:, None]
    )
    return (jnp.where(allowed[None], raw, -1e30), allowed)


QG = 4
LOG2E = 1.4426950408889634
LN2 = 0.6931471805599453
T = 1024
MC = 8


class Place:
    def __init__(self):
        wide, narrow = lax.axis_index("wide"), lax.axis_index("narrow")
        self.z, self.x = wide // 2, wide % 2
        self.y, self.c = narrow // 2, narrow % 2
        self.me = (self.z, self.x, self.y, self.c)
        self.zs = [(self.z + d) % 4 for d in (1, 2, 3)]

    def device(self, z, x, y, c):
        return (z * 2 + x, y * 2 + c)

    def targets(self, axis):
        z, x, y, c = self.me
        if axis == "z":
            return [(i, (other, x, y, c)) for i, other in enumerate(self.zs)]
        return [
            {"x": (3, (z, 1 - x, y, c)), "y": (4, (z, x, 1 - y, c)), "c": (5, (z, x, y, 1 - c))}[axis]
        ]

    def partners(self):
        z, x, y, c = self.me
        return [self.device(p, x, y, c) for p in self.zs] + [
            self.device(z, 1 - x, y, c),
            self.device(z, x, 1 - y, c),
            self.device(z, x, y, 1 - c),
        ]

    def greet(self):
        barrier = pltpu.get_barrier_semaphore()
        for other in self.partners():
            pl.semaphore_signal(barrier, inc=1, device_id=other, device_id_type=MESH)
        pl.semaphore_wait(barrier, 6)


def dg(a, b, ca, cb):
    return lax.dot_general(a, b, (((ca,), (cb,)), ((), ())), preferred_element_type=f32)


def exact(a, b, ca, cb):
    return lax.dot_general(
        a, b, (((ca,), (cb,)), ((), ())), precision=lax.Precision.HIGHEST,
        preferred_element_type=f32,
    )


def remote(src, dst, send, recv, device):
    return pltpu.make_async_remote_copy(
        src_ref=src, dst_ref=dst, send_sem=send, recv_sem=recv,
        device_id=device, device_id_type=MESH,
    )


class Gather:
    def __init__(self, place, view, order, send, recv):
        self.p, self.view, self.axes = place, view, order + "c"
        self.send, self.recv = send, recv

    def copies(self, i):
        me, axis = self.p.me, self.axes[i]
        part = [ALL if a in self.axes[:i] else me["zxyc".index(a)] for a in "zxyc"]
        return [
            remote(
                self.view(*part), self.view(*part), self.send(slot), self.recv(slot),
                self.p.device(*to),
            )
            for slot, to in self.p.targets(axis)
        ]

    def step(self, i):
        if i > 0:
            for copy in self.copies(i - 1):
                copy.wait_recv()
        if i < 4:
            for copy in self.copies(i):
                copy.start()

    def close(self):
        for i in range(4):
            for copy in self.copies(i):
                copy.wait_send()


class Scatter:
    def __init__(self, place, part, bufs, order, send, recv):
        self.p, self.part, self.bufs = place, part, bufs
        self.axes = "c" + order[::-1]
        self.send, self.recv = send, recv

    def index(self, i, value):
        return [
            value if a == self.axes[i] else (self.p.me[k] if a in self.axes[:i] else ALL)
            for k, a in enumerate("zxyc")
        ]

    def landing(self, i):
        buf = self.bufs[i]
        return [buf.at[n] for n in range(3)] if self.axes[i] == "z" else [buf]

    def copies(self, i):
        at = "zxyc".index(self.axes[i])
        return [
            remote(
                self.part(*self.index(i, to[at])), land, self.send(slot), self.recv(slot),
                self.p.device(*to),
            )
            for land, (slot, to) in zip(self.landing(i), self.p.targets(self.axes[i]))
        ]

    def step(self, i):
        if i > 0:
            for copy in self.copies(i - 1):
                copy.wait_recv()
            part = self.part(*self.index(i - 1, self.p.me["zxyc".index(self.axes[i - 1])]))
            for buf in self.landing(i - 1):
                part[...] = part[...] + buf[...]
        for copy in self.copies(i):
            copy.start()

    def total(self):
        for copy in self.copies(3):
            copy.wait_recv()
        out = self.part(*self.p.me)[...].astype(f32)
        for buf in self.landing(3):
            out = out + buf[...].astype(f32)
        for i in range(4):
            for copy in self.copies(i):
                copy.wait_send()
        return out


def begins(ends, t):
    first = jnp.zeros_like(t)
    for e in ends:
        first = jnp.where(t >= e, e, first)
    return first


def tables(ends, cos_ref, up_ref, down_ref):
    t = lax.broadcasted_iota(jnp.int32, (T, 128), 0)
    d = lax.broadcasted_iota(jnp.int32, (T, 128), 1) % 64
    offset = (t - begins(ends, t)).astype(f32)
    freq = jnp.exp((d % 8).astype(f32) * (-2.0 / 16 * 9.210340371976184))
    angle = offset * freq
    cos, sin = jnp.cos(angle), jnp.sin(angle)
    cos_ref[...] = jnp.where(d < 16, cos, 1.0)
    up_ref[...] = jnp.where(d < 8, -sin, 0.0)
    down_ref[...] = jnp.where((d >= 8) & (d < 16), sin, 0.0)


def turn(v, cos, up, down, sign):
    out = []
    for i in range(2):
        w = v[:, 128 * i : 128 * (i + 1)]
        r = pltpu.roll(w, 120, 1) * up + pltpu.roll(w, 8, 1) * down
        out.append(w * cos + r if sign > 0 else w * cos - r)
    return jnp.concatenate(out, axis=1)


def attention_group(flag, hid, g, W, Wo, bias, tabs, bufs, attT, dqkv, pump):
    q_s, k_s, v_s, qT, kT, vT, doT, E, DS, dv, dk, dqT = bufs
    R = 512
    for i in range(T // R):
        rows = pl.ds(i * R, R)
        tb = [t[rows, :] for t in tabs]
        h = hid[rows, :]
        q = turn(dg(h, W(0), 1, 0) + bias(0), *tb, 1) * (LOG2E / 8)
        q = q.astype(bf16)
        q_s[rows, :] = q
        qT[:, rows] = q.T
        k = turn(dg(h, W(1), 1, 0) + bias(1), *tb, 1).astype(bf16)
        k_s[rows, :] = k
        kT[:, rows] = k.T
        v = (dg(h, W(2), 1, 0) + bias(2)).astype(bf16)
        v_s[rows, :] = v
        vT[:, rows] = v.T
    pump(0)
    for i in range(T // R):
        rows = pl.ds(i * R, R)
        do = dg(g[rows, :], Wo, 1, 1).astype(bf16)
        doT[:, rows] = do.T
    head_row = lax.broadcasted_iota(jnp.int32, (256, 256), 0) // 64
    head_lane = lax.broadcasted_iota(jnp.int32, (256, 256), 1) // 64
    causal = lax.broadcasted_iota(jnp.int32, (256, 256), 0) <= lax.broadcasted_iota(
        jnp.int32, (256, 256), 1
    )
    for qb in range(T // 256):
        kk = 256 * (qb + 1)
        cols = pl.ds(256 * qb, 256)

        def head(h):
            hc, hr = pl.ds(h * 256, 256), pl.ds(h * 64, 64)
            s = dg(k_s[0:kk, :], jnp.where(head_row == h, qT[:, cols], 0), 1, 0)
            blocks = [s[256 * b : 256 * (b + 1)] for b in range(qb + 1)]
            blocks[qb] = jnp.where(causal, blocks[qb], -1e30)
            m = jnp.max(blocks[qb], axis=0, keepdims=True)
            for b in range(qb):
                top = jnp.max(blocks[b], axis=0, keepdims=True)
                m = jnp.maximum(m, jnp.where(flag(b, qb), top, -1e30))
            total = None
            for b in range(qb + 1):
                e = jnp.exp2(blocks[b] - (m if b == qb else jnp.where(flag(b, qb), m, 1e30)))
                t = jnp.sum(e, axis=0, keepdims=True)
                total = t if total is None else total + t
                E[256 * b : 256 * (b + 1), hc] = e.astype(bf16)
            inv = 1.0 / total
            oT = dg(vT[hr, 0:kk], E[0:kk, hc], 1, 0) * inv
            attT[hr, cols] = oT.astype(bf16)
            dot = jnp.sum(doT[hr, cols].astype(f32) * oT, axis=0, keepdims=True) * inv
            doz = jnp.where(head_row == h, doT[:, cols].astype(f32) * inv, 0.0).astype(bf16)
            dp = dg(v_s[0:kk, :], doz, 1, 0)
            DS[0:kk, hc] = (E[0:kk, hc].astype(f32) * (dp - dot)).astype(bf16)
            dqT[hr, cols] = dg(kT[hr, 0:kk], DS[0:kk, hc], 1, 0)
            return doz.T

        doz = jnp.concatenate([head(h) for h in range(4)], axis=0)
        q = q_s[cols, :]
        qz = jnp.concatenate([jnp.where(head_lane == h, q, 0) for h in range(4)], axis=0)
        pv = dg(E[0:kk, :], doz, 1, 0)
        pk = dg(DS[0:kk, :], qz, 1, 0)
        if qb > 0:
            dv[0 : 256 * qb, :] += pv[0 : 256 * qb]
            dk[0 : 256 * qb, :] += pk[0 : 256 * qb]
        dv[256 * qb : kk, :] = pv[256 * qb :]
        dk[256 * qb : kk, :] = pk[256 * qb :]
        pump(qb + 1)
    for i in range(T // R):
        rows = pl.ds(i * R, R)
        tb = [t[rows, :] for t in tabs]
        dqkv[rows, 0:256] = turn(dqT[:, rows].T * 0.125, *tb, -1).astype(bf16)
        dqkv[rows, 256:512] = turn(dk[rows, :] * LN2, *tb, -1).astype(bf16)
        dqkv[rows, 512:768] = dv[rows, :].astype(bf16)


def gelu_parts(x):
    a1, a2, a3, a4, a5 = 0.254829592, -0.284496736, 1.421413741, -1.453152027, 1.061405429
    ex = jnp.exp2(x * x * (-0.5 * LOG2E))
    t = 1.0 / (1.0 + (0.3275911 * 0.7071067811865476) * jnp.abs(x))
    half = ((((0.5 * a5 * t + 0.5 * a4) * t + 0.5 * a3) * t + 0.5 * a2) * t + 0.5 * a1) * t * ex
    phi = jnp.where(x < 0, half, 1.0 - half)
    return x * phi, phi + x * ex * 0.3989422804014327


def spread(kind, width):
    lane = lax.broadcasted_iota(jnp.int32, (128, width), 0)
    at = lax.broadcasted_iota(jnp.int32, (128, width), 1)
    col = lax.broadcasted_iota(jnp.int32, (32, width), 1)
    rank = lax.broadcasted_iota(jnp.int32, (32, width), 0)
    if kind == "qkv":
        return lane == at % 96, col // 96 == rank
    if kind == "fc_in":
        return lane == at // 512 * 16 + at % 16, col % 512 // 16 == rank
    return lane == at % 32 + 32 * kind, col // 32 == rank


def from_ranks(rows, kind, width):
    hot, mine = spread(kind, width)
    t = dg(rows, jnp.where(hot, 1.0, 0.0).astype(bf16), 1, 0)
    return jnp.sum(jnp.where(mine, t, 0.0), axis=0, keepdims=True)


def to_ranks(vector, kind, width):
    hot, mine = spread(kind, width)
    return exact(jnp.where(mine, vector, 0.0), jnp.where(hot, 1.0, 0.0), 1, 1)


def normalised(x):
    centred = x - jnp.mean(x, axis=-1, keepdims=True)
    inverse = lax.rsqrt(jnp.mean(centred * centred, axis=-1, keepdims=True) + epsilon)
    return centred * inverse, inverse


NP = 3
NR = 2


def lanes(start, size):
    return pl.ds(pl.multiple_of(start, 128), size)


def layer_kernel(
    lens, tokens, cot, qkv, out, fc_in, down, small,
    mixed, tokens_grad, out_q, out_o, out_i, out_d, out_s, stats,
    ag_q, ag_o, ag_i, ag_d, ag_s,
    hid, hidT, g, hgrad, attT, vecs, gvecs, wide_b, wide_g, sv,
    cos, up, turn_down, wo, wq, wd, dqkv, q_s, k_s, v_s, qT, kT, vT, doT, E, DS, mlp, dqT,
    part, r1, r2, r3, rz, part_s, s1, s2, s3, sz,
    own, io, fetch, send, recv, gsend, grecv,
):
    place = Place()
    me = place.me

    def gather(n, views, orders=("zxy", "zyx")):
        return [
            Gather(place, view, order, lambda s, k=k: gsend.at[n, k, s], lambda s, k=k: grecv.at[n, k, s])
            for k, (view, order) in enumerate(zip(views, orders))
        ]

    def gather_q(i):
        return gather(
            i, [lambda *a, h=h: ag_q.at[(i,) + a + (pl.ds(16 * h, 16),)] for h in range(2)]
        )

    def gather_o():
        return gather(4, [lambda *a, h=h: ag_o.at[a + (pl.ds(16 * h, 16),)] for h in range(2)])

    def gather_m(j):
        return gather(5 + j, [lambda *a: ag_i.at[(j,) + a], lambda *a: ag_d.at[(j,) + a]])

    def step(arrays, i):
        for array in arrays:
            array.step(i)

    vectors = gather(13, [lambda *a: ag_s.at[a]])

    def sums(n, width):
        return [
            Scatter(
                place,
                lambda *a, k=k: part.at[(k, n % NP) + a + (ALL, pl.ds(0, width))],
                [
                    b.at[(k, n % NR) + (ALL,) * d + (ALL, pl.ds(0, width))]
                    for b, d in ((r1, 3), (r2, 2), (r3, 1), (rz, 1))
                ],
                ("zxy", "zyx")[k],
                lambda s, k=k: send.at[n, k, s],
                lambda s, k=k: recv.at[n, k, s],
            )
            for k in range(2)
        ]

    def end_q(i):
        totals = [array.total() for array in sums(i, 768)]
        for h in range(2):
            for j in range(3):
                out_q[pl.ds(16 * h, 16), lanes(1024 * j + 256 * i, 256)] = totals[h][
                    :, 256 * j : 256 * (j + 1)
                ]

    def end_m(n):
        totals = [array.total() for array in sums(n, 1024)]

        @pl.when(n == 4)
        def _():
            for h in range(2):
                out_o[pl.ds(16 * h, 16), :] = totals[h]

        @pl.when(n > 4)
        def _():
            j = jnp.maximum(n - 5, 0)
            for h in range(2):
                out_i[pl.ds(16 * h, 16), lanes(512 * j, 512)] = totals[0][
                    :, 512 * h : 512 * (h + 1)
                ]
            out_d[pl.ds(pl.multiple_of(16 * j, 16), 16), :] = totals[1]

    own_copies = []

    def own_copy(src, dst):
        copy = pltpu.make_async_copy(src, dst, own.at[len(own_copies)])
        copy.start()
        own_copies.append(copy)
        return copy

    own_copy(small, ag_s.at[me])
    for i in range(QG):
        for j in range(3):
            own_copy(
                qkv.at[:, pl.ds(1024 * j + 256 * i, 256)],
                ag_q.at[(i,) + me + (ALL, pl.ds(256 * j, 256))],
            )
        if i == 0:
            own_copy(out, ag_o.at[me])
    for j in range(MC):
        own_copy(fc_in.at[:, pl.ds(512 * j, 512)], ag_i.at[(j,) + me])
        own_copy(down.at[pl.ds(16 * j, 16)], ag_d.at[(j,) + me])
    load_x = pltpu.make_async_copy(tokens, attT, io.at[0])
    load_x.start()
    load_g = pltpu.make_async_copy(cot, g, io.at[1])
    load_g.start()
    place.greet()
    own_copies[0].wait()
    step(vectors, 0)
    for copy in own_copies[1:5]:
        copy.wait()
    q0, o = gather_q(0), gather_o()
    step(q0, 0)
    step(o, 0)
    for copy in own_copies[5:]:
        copy.wait()
    ends = [lens[0, 0], lens[0, 0] + lens[0, 1], lens[0, 0] + lens[0, 1] + lens[0, 2]]

    def flag(b, qb):
        return 256 * b >= begins(ends, jnp.full((1, 256), 256 * qb, jnp.int32))

    tables(ends, cos, up, turn_down)
    step(vectors, 1)
    step(q0, 1)
    step(vectors, 2)
    step(gather_q(1), 0)
    step(vectors, 3)
    step(o, 1)
    step(vectors, 4)
    load_s = pltpu.make_async_copy(ag_s, sv, io.at[2])
    load_s.start()
    step(q0, 2)
    load_s.wait()
    rows = sv[...].reshape(32, 8, 128)
    row0, row1, row2 = (rows[:, i, :].astype(bf16) for i in range(3))
    for i in range(4):
        vecs[i : i + 1, :] = from_ranks(row0, i, 1024)
    wide_b[0:1, 0:3072] = from_ranks(row1, "qkv", 3072)
    wide_b[1:2, :] = from_ranks(row2, "fc_in", 4096)
    step(o, 2)
    step(gather_m(0), 0)
    step(gather_m(1), 0)
    step(q0, 3)
    load_x.wait()
    for i in range(4):
        rows = pl.ds(256 * i, 256)
        normed, _ = normalised(attT[rows, :].astype(f32))
        h = (normed * vecs[0:1, :] + vecs[1:2, :]).astype(bf16)
        hid[rows, :] = h
        hidT[:, rows] = h.T
    hgrad[...] = jnp.zeros_like(hgrad)
    step(q0, 4)

    def fetch_q(i):
        return pltpu.make_async_copy(ag_q.at[i], wq.at[i % 2], fetch.at[i % 2])

    fetch_q(0).start()
    step(o, 3)
    step(o, 4)
    fetch_o = pltpu.make_async_copy(ag_o, wo, fetch.at[2])
    fetch_o.start()
    load_g.wait()
    fetch_o.wait()

    bufs = (
        q_s, k_s, v_s, qT, kT, vT, doT, E, DS,
        mlp.at[:, pl.ds(0, 256)], mlp.at[:, pl.ds(256, 256)], dqT,
    )

    def attention_step(i, carry):
        fetch_q(i).wait()
        more, before = i < QG - 1, i > 0
        a, b = gather_m(2 * i), gather_m(2 * i + 1)

        @pl.when(more)
        def _():
            step(gather_q(i + 1), 1)

            @pl.when(i < QG - 2)
            def _():
                step(gather_q(i + 2), 0)

        step(a, 1)

        def pump(p):
            if p == 0:
                step(b, 1)

                @pl.when(before)
                def _():
                    step(sums(i - 1, 768), 1)

                @pl.when(more)
                def _():
                    step(gather_m(2 * i + 2), 0)

            elif p == 1:

                @pl.when(more)
                def _():
                    step(gather_q(i + 1), 2)
                    step(gather_m(2 * i + 3), 0)

            elif p == 2:
                step(a, 2)

                @pl.when(before)
                def _():
                    step(sums(i - 1, 768), 2)

            elif p == 3:

                @pl.when(more)
                def _():
                    step(gather_q(i + 1), 3)

                step(b, 2)
            elif p == 4:
                step(a, 3)

                @pl.when(more)
                def _():
                    step(gather_q(i + 1), 4)
                    fetch_q(i + 1).start()

                @pl.when(before)
                def _():
                    step(sums(i - 1, 768), 3)

            elif p == 5:
                step(b, 3)
            else:
                step(a, 4)
                step(b, 4)

                @pl.when(before)
                def _():
                    end_q(i - 1)

        def W(j):
            return wq[i % 2, :, :, :, :, :, 256 * j : 256 * (j + 1)].reshape(T, 256)

        def bias(j):
            return wide_b[0:1, lanes(1024 * j + 256 * i, 256)]

        attention_group(
            flag, hid, g, W, wo[i].reshape(256, T), bias, (cos, up, turn_down), bufs,
            attT.at[pl.ds(pl.multiple_of(256 * i, 256), 256)], dqkv, pump,
        )
        for b_ in range(2):
            v = dg(hidT[512 * b_ : 512 * (b_ + 1), :], dqkv[...], 1, 0).astype(bf16)
            v = v.reshape(2, 2, 2, 2, 2, 16, 768)
            for h in range(2):
                part[h, i % NP, 2 * b_ : 2 * b_ + 2, :, :, :, :, 0:768] = v[:, :, :, :, h]
        step(sums(i, 768), 0)
        pump(5)
        total = jnp.sum(dqkv[...].astype(f32), axis=0, keepdims=True)
        for j in range(3):
            wide_g[0:1, lanes(1024 * j + 256 * i, 256)] = total[:, 256 * j : 256 * (j + 1)]
        whole_w = wq[i % 2].reshape(T, 768)
        for b_ in range(2):
            rows = pl.ds(512 * b_, 512)
            hgrad[rows, :] += dg(dqkv[rows, :], whole_w, 1, 1)
        pump(6)
        return carry

    lax.fori_loop(0, QG, attention_step, 0)

    def fetch_m(j):
        return [
            pltpu.make_async_copy(
                ag_i.at[j], wq.at[j % 2, :, :, :, :, :, pl.ds(0, 512)], fetch.at[j % 2]
            ),
            pltpu.make_async_copy(ag_d.at[j], wd.at[j % 2], fetch.at[2 + j % 2]),
        ]

    for copy in fetch_m(0):
        copy.start()
    step(sums(3, 768), 1)
    for b in range(2):
        v = dg(attT[512 * b : 512 * (b + 1), :], g[...], 1, 0).astype(bf16)
        v = v.reshape(2, 2, 2, 2, 2, 16, T)
        for h in range(2):
            part[h, 4 % NP, 2 * b : 2 * b + 2] = v[:, :, :, :, h]
    step(sums(4, 1024), 0)
    step(sums(3, 768), 2)
    step(sums(4, 1024), 1)
    step(sums(3, 768), 3)
    mlp[...] = jnp.zeros_like(mlp)
    end_q(3)

    act, pg = DS.at[:, pl.ds(0, 512)], DS.at[:, pl.ds(512, 512)]

    def mlp_step(j, carry):
        for copy in fetch_m(j):
            copy.wait()

        @pl.when(j < MC - 1)
        def _():
            for copy in fetch_m(j + 1):
                copy.start()

        w_in = wq[j % 2, :, :, :, :, :, 0:512].reshape(T, 512)
        w_down = wd[j % 2].reshape(512, T)
        bias = wide_b[1:2, lanes(512 * j, 512)]
        for b in range(2):
            rows = pl.ds(512 * b, 512)
            pre = dg(hid[rows, :], w_in, 1, 0) + bias
            a, d = gelu_parts(pre)
            act[rows, :] = a.astype(bf16)
            pg[rows, :] = (dg(g[rows, :], w_down, 1, 1) * d).astype(bf16)
        wide_g[1:2, lanes(512 * j, 512)] = jnp.sum(pg[...].astype(f32), axis=0, keepdims=True)

        @pl.when(j > 0)
        def _():
            end_m(j + 3)

        slot = (j + 5) % NP
        for b in range(2):
            v = dg(hidT[512 * b : 512 * (b + 1), :], pg[...], 1, 0).astype(bf16)
            v = v.reshape(2, 2, 2, 2, 2, 16, 512)
            for h in range(2):
                part[0, slot, 2 * b : 2 * b + 2, :, :, :, :, 512 * h : 512 * (h + 1)] = v[
                    :, :, :, :, h
                ]
            v = dg(act[:, 256 * b : 256 * (b + 1)], g[...], 0, 0).astype(bf16)
            part[1, slot, 2 * b : 2 * b + 2] = v.reshape(2, 2, 2, 2, 16, T)
        step(sums(j + 5, 1024), 0)
        step(sums(j + 4, 1024), 2)
        for b in range(2):
            rows = pl.ds(512 * b, 512)
            mlp[rows, :] += dg(act[rows, :], w_down, 1, 0)
            hgrad[rows, :] += dg(pg[rows, :], w_in, 1, 1)
        step(sums(j + 5, 1024), 1)
        step(sums(j + 4, 1024), 3)
        return carry

    lax.fori_loop(0, MC, mlp_step, 0)

    last = MC + 4
    reload_x = pltpu.make_async_copy(tokens, hid, io.at[0])
    reload_x.start()
    reload_x.wait()
    for i in range(4):
        rows = pl.ds(256 * i, 256)
        normed, inverse = normalised(hid[rows, :].astype(f32))
        h = hgrad[rows, :]
        up_g = g[rows, :].astype(f32)
        for k, v in enumerate((h * normed, h, up_g)):
            v = jnp.sum(v, axis=0, keepdims=True)
            gvecs[k : k + 1, :] = v if i == 0 else gvecs[k : k + 1, :] + v
        n = h * vecs[0:1, :]
        d = n - jnp.mean(n, axis=-1, keepdims=True)
        d = d - normed * jnp.mean(n * normed, axis=-1, keepdims=True)
        hidT[rows, :] = (up_g + inverse * d).astype(bf16)
    put_tg = pltpu.make_async_copy(hidT, tokens_grad, io.at[1])
    put_tg.start()
    step(sums(last, 1024), 2)
    end_m(jnp.int32(last - 1))
    row0 = sum(to_ranks(gvecs[min(k, 2) : min(k, 2) + 1, :], k, 1024) for k in range(4))
    row1 = to_ranks(wide_g[0:1, 0:3072], "qkv", 3072)
    row2 = to_ranks(wide_g[1:2, :], "fc_in", 4096)
    for r in range(32):
        part_s[r // 8, r // 4 % 2, r // 2 % 2, r % 2] = jnp.concatenate(
            [row0[r : r + 1], row1[r : r + 1], row2[r : r + 1], jnp.zeros((5, 128), f32)]
        )
    tiny = Scatter(
        place, lambda *a: part_s.at[a], [s1, s2, s3, sz], "zxy",
        lambda s: send.at[13, 0, s], lambda s: recv.at[13, 0, s],
    )
    tiny.step(0)
    step(sums(last, 1024), 3)
    tiny.step(1)
    w_out = wo[...].reshape(T, T)
    squares = [jnp.zeros((1, T), f32)] * 3
    for i in range(4):
        rows = pl.ds(256 * i, 256)
        x = hid[rows, :].astype(f32)
        a = dg(attT[:, rows], w_out, 0, 0) + vecs[2:3, :]
        m = mlp[rows, :] + vecs[3:4, :]
        hid[rows, :] = (x + a + m).astype(bf16)
        squares = [
            s + jnp.sum(v * v, axis=0, keepdims=True) for s, v in zip(squares, (x, a, m))
        ]
        if i == 1:
            tiny.step(2)
    put_mixed = pltpu.make_async_copy(hid, mixed, io.at[0])
    put_mixed.start()
    tiny.step(3)
    for i in range(3):
        total = jnp.sum(squares[i], axis=1, keepdims=True)
        stats[i : i + 1, :] = jnp.broadcast_to(total, (1, 128))
    end_m(jnp.int32(last))
    out_s[...] = tiny.total()
    put_tg.wait()
    put_mixed.wait()
    for arrays in [vectors, o] + [gather_q(i) for i in range(QG)]:
        for array in arrays:
            array.close()

    def close_m(j, carry):
        for array in gather_m(j):
            array.close()
        return carry

    lax.fori_loop(0, MC, close_m, 0)


def whole_layer(lens, tokens, cot, qkv, out, fc_in, down, small):
    any_ = pl.BlockSpec(memory_space=pl.ANY)
    vmem = pl.BlockSpec(memory_space=pltpu.VMEM)
    sd = jax.ShapeDtypeStruct
    ranks = (4, 2, 2, 2)
    dma = pltpu.SemaphoreType.DMA
    return pl.pallas_call(
        layer_kernel,
        out_shape=[
            sd((T, T), bf16),
            sd((T, T), bf16),
            sd((32, 3072), f32),
            sd((32, 1024), f32),
            sd((32, 4096), f32),
            sd((128, 1024), f32),
            sd((8, 128), f32),
            sd((8, 128), f32),
            sd((QG,) + ranks + (32, 768), bf16),
            sd(ranks + (32, 1024), bf16),
            sd((MC,) + ranks + (32, 512), bf16),
            sd((MC,) + ranks + (16, 1024), bf16),
            sd(ranks + (8, 128), f32),
        ],
        in_specs=[pl.BlockSpec(memory_space=pltpu.SMEM)] + [any_] * 7,
        out_specs=[any_] * 2 + [vmem] * 6 + [any_] * 5,
        scratch_shapes=[
            pltpu.VMEM((T, T), bf16),
            pltpu.VMEM((T, T), bf16),
            pltpu.VMEM((T, T), bf16),
            pltpu.VMEM((T, T), f32),
            pltpu.VMEM((T, T), bf16),
            pltpu.VMEM((8, 1024), f32),
            pltpu.VMEM((8, 1024), f32),
            pltpu.VMEM((8, 4096), f32),
            pltpu.VMEM((8, 4096), f32),
            pltpu.VMEM(ranks + (8, 128), f32),
            pltpu.VMEM((T, 128), f32),
            pltpu.VMEM((T, 128), f32),
            pltpu.VMEM((T, 128), f32),
            pltpu.VMEM(ranks + (32, 1024), bf16),
            pltpu.VMEM((2,) + ranks + (32, 768), bf16),
            pltpu.VMEM((2,) + ranks + (16, 1024), bf16),
            pltpu.VMEM((T, 768), bf16),
            pltpu.VMEM((T, 256), bf16),
            pltpu.VMEM((T, 256), bf16),
            pltpu.VMEM((T, 256), bf16),
            pltpu.VMEM((256, T), bf16),
            pltpu.VMEM((256, T), bf16),
            pltpu.VMEM((256, T), bf16),
            pltpu.VMEM((256, T), bf16),
            pltpu.VMEM((T, T), bf16),
            pltpu.VMEM((T, T), bf16),
            pltpu.VMEM((T, T), f32),
            pltpu.VMEM((256, T), f32),
            pltpu.VMEM((2, NP) + ranks + (16, 1024), bf16),
            pltpu.VMEM((2, NR, 4, 2, 2, 16, 1024), bf16),
            pltpu.VMEM((2, NR, 4, 2, 16, 1024), bf16),
            pltpu.VMEM((2, NR, 4, 16, 1024), bf16),
            pltpu.VMEM((2, NR, 3, 16, 1024), bf16),
            pltpu.VMEM(ranks + (8, 128), f32),
            pltpu.VMEM((4, 2, 2, 8, 128), f32),
            pltpu.VMEM((4, 2, 8, 128), f32),
            pltpu.VMEM((4, 8, 128), f32),
            pltpu.VMEM((3, 8, 128), f32),
            dma((30,)),
            dma((3,)),
            dma((4,)),
            dma((14, 2, 6)),
            dma((14, 2, 6)),
            dma((14, 2, 6)),
            dma((14, 2, 6)),
        ],
        compiler_params=pltpu.CompilerParams(
            collective_id=0, has_side_effects=True, vmem_limit_bytes=63 * 2**20
        ),
    )(lens, tokens, cot, qkv, out, fc_in, down, small)


def layer_math(
    tokens, cotangent, seq_lens, gain, shift, qkv_matrix, qkv_b, out_matrix, out_b,
    in_matrix, in_b, down_matrix, down_b,
):
    gain_full, shift_full = gain.astype(f32), shift.astype(f32)
    row_count, width = tokens.shape
    inputs = tokens.astype(f32)
    centred = inputs - jnp.mean(inputs, axis=-1, keepdims=True)
    inverse = lax.rsqrt(jnp.mean(centred * centred, axis=-1, keepdims=True) + epsilon)
    normed = centred * inverse
    hid_low = (normed * gain_full + shift_full).astype(bf16)
    qkv = jnp.dot(hid_low, qkv_matrix, preferred_element_type=f32) + qkv_b.astype(f32)
    segment, places, offset = positions(seq_lens[0], row_count)
    freqs = 10000.0 ** (-jnp.arange(ROT // 2, dtype=f32) * 2.0 / ROT)
    angle = offset[:, None] * freqs[None, :]
    cosine = jnp.cos(angle)[:, None, :]
    sine = jnp.sin(angle)[:, None, :]
    heads = (row_count, HEADS, HEAD)
    q_low = rotate(qkv[:, :width].reshape(heads), cosine, sine).astype(bf16)
    k_low = rotate(qkv[:, width : 2 * width].reshape(heads), cosine, sine).astype(bf16)
    v_low = qkv[:, 2 * width :].reshape(heads).astype(bf16)
    block_rows = min(512, row_count)
    block_count = row_count // block_rows
    outputs = []
    kept_lse = []
    for block in range(block_count):
        lower = block * block_rows
        upper = lower + block_rows
        scores, allowed = block_scores(
            q_low[lower:upper], k_low[:upper], segment[lower:upper], segment[:upper],
            places[lower:upper], places[:upper],
        )
        row_max = jnp.max(scores, axis=-1, keepdims=True)
        expo = jnp.exp(scores - row_max)
        totals = jnp.sum(expo, axis=-1, keepdims=True)
        soft_low = (expo / totals).astype(bf16)
        kept_lse.append(row_max + jnp.log(totals))
        outputs.append(
            jnp.einsum("hqk,khd->qhd", soft_low, v_low[:upper], preferred_element_type=f32)
        )
    att_low = jnp.concatenate(outputs, axis=0).reshape(row_count, width).astype(bf16)
    attn_out = jnp.dot(att_low, out_matrix, preferred_element_type=f32) + out_b.astype(f32)
    pre = jnp.dot(hid_low, in_matrix, preferred_element_type=f32) + in_b.astype(f32)
    gelu_exact = partial(jax.nn.gelu, approximate=False)
    act_low = gelu_exact(pre).astype(bf16)
    mlp = jnp.dot(act_low, down_matrix, preferred_element_type=f32) + down_b.astype(f32)
    mixed = (inputs + attn_out + mlp).astype(bf16)
    stream_rms = jnp.sqrt(
        jnp.stack([jnp.mean(inputs * inputs), jnp.mean(attn_out * attn_out), jnp.mean(mlp * mlp)])
    )[None, :]
    upstream = cotangent.astype(f32)
    grad_down = transposed_times(act_low, cotangent)
    grad_out = transposed_times(att_low, cotangent)
    grad_sum = jnp.sum(upstream, axis=0)
    act_grad = times_transposed(cotangent, down_matrix)
    _, gelu_pull = jax.vjp(gelu_exact, pre)
    pre_grad_low = gelu_pull(act_grad)[0].astype(bf16)
    grad_in = transposed_times(hid_low, pre_grad_low)
    grad_in_b = jnp.sum(pre_grad_low.astype(f32), axis=0)
    att_grad_low = times_transposed(cotangent, out_matrix).astype(bf16).reshape(heads)
    query_grads = []
    key_grad = jnp.zeros(heads, f32)
    value_grad = jnp.zeros(heads, f32)
    for block in range(block_count):
        lower = block * block_rows
        upper = lower + block_rows
        query_block = q_low[lower:upper]
        scores, allowed = block_scores(
            query_block, k_low[:upper], segment[lower:upper], segment[:upper],
            places[lower:upper], places[:upper],
        )
        soft = jnp.where(allowed[None], jnp.exp(scores - kept_lse[block]), 0.0)
        soft_low = soft.astype(bf16)
        out_grad = att_grad_low[lower:upper]
        value_part = jnp.einsum("hqk,qhd->khd", soft_low, out_grad, preferred_element_type=f32)
        prob_grad = jnp.einsum("qhd,khd->hqk", out_grad, v_low[:upper], preferred_element_type=f32)
        score_grad = soft * (prob_grad - jnp.sum(soft * prob_grad, axis=-1, keepdims=True))
        score_low = score_grad.astype(bf16)
        query_grads.append(
            jnp.einsum("hqk,khd->qhd", score_low, k_low[:upper], preferred_element_type=f32)
            * HEAD ** (-0.5)
        )
        key_part = jnp.einsum(
            "hqk,qhd->khd", score_low, query_block, preferred_element_type=f32
        ) * HEAD ** (-0.5)
        padding = ((0, row_count - upper), (0, 0), (0, 0))
        key_grad = key_grad + jnp.pad(key_part, padding)
        value_grad = value_grad + jnp.pad(value_part, padding)
    query_grad = unrotate(jnp.concatenate(query_grads, axis=0), cosine, sine)
    key_grad = unrotate(key_grad, cosine, sine)
    qkv_grad_low = jnp.concatenate(
        [g.reshape(row_count, width) for g in (query_grad, key_grad, value_grad)], axis=1
    ).astype(bf16)
    grad_qkv = transposed_times(hid_low, qkv_grad_low)
    grad_qkv_b = jnp.sum(qkv_grad_low.astype(f32), axis=0)
    hidden_grad = times_transposed(qkv_grad_low, qkv_matrix) + times_transposed(
        pre_grad_low, in_matrix
    )
    grad_gain = jnp.sum(hidden_grad * normed, axis=0)
    grad_shift = jnp.sum(hidden_grad, axis=0)
    scaled = hidden_grad * gain_full
    input_grad = upstream + inverse * (
        scaled
        - jnp.mean(scaled, axis=-1, keepdims=True)
        - normed * jnp.mean(scaled * normed, axis=-1, keepdims=True)
    )
    return (
        mixed, input_grad.astype(bf16), grad_gain, grad_shift, grad_qkv, grad_qkv_b,
        grad_out, grad_sum, grad_in, grad_in_b, grad_down, grad_sum, stream_rms,
    )


def generic(tokens, cotangent, seq_lens, *shards):
    axes = ("wide", "narrow")
    whole = [lax.all_gather(s, axes, axis=0, tiled=True) for s in shards]
    results = layer_math(tokens, cotangent, seq_lens, *whole)
    summed = [
        lax.psum_scatter(g, axes, scatter_dimension=0, tiled=True) for g in results[2:12]
    ]
    return (*results[:2], *summed, results[12])


def local(
    tokens, cotangent, seq_lens, norm_gain, norm_bias, qkv_weight, qkv_bias, out_weight,
    out_bias, fc_in_weight, fc_in_bias, fc_out_weight, fc_out_bias,
):
    in_mixed = fc_in_weight.reshape(32, 32, MC, 16).transpose(0, 2, 1, 3).reshape(32, 4096)
    row0 = jnp.concatenate([norm_gain, norm_bias, out_bias, fc_out_bias])
    row1 = jnp.pad(qkv_bias, (0, 32))
    small = jnp.stack([row0, row1, fc_in_bias] + [jnp.zeros_like(row0)] * 5).astype(f32)
    mixed, tokens_grad, out_q, out_o, out_i, out_d, out_s, stats, *_ = whole_layer(
        seq_lens, tokens, cotangent, qkv_weight, out_weight, in_mixed, fc_out_weight, small
    )
    out_i = out_i.reshape(32, MC, 32, 16).transpose(0, 2, 1, 3).reshape(32, 4096)
    stream_rms = jnp.sqrt(stats[0:3, 0] / (tokens.shape[0] * tokens.shape[1]))[None, :]
    return (
        mixed, tokens_grad, out_s[0, :32], out_s[0, 32:64], out_q, out_s[1, :96], out_o,
        out_s[0, 64:96], out_i, out_s[2], out_d, out_s[0, 96:], stream_rms,
    )


def solution(mesh):
    rows, flat = P(("wide", "narrow"), None), P(("wide", "narrow"))
    fits = mesh.shape["wide"] == 8 and mesh.shape["narrow"] == 4
    return jax.shard_map(
        local if fits else generic,
        mesh=mesh,
        in_specs=(rows, rows, rows, flat, flat, rows, flat, rows, flat, rows, flat, rows, flat),
        out_specs=(rows, rows, flat, flat, rows, flat, rows, flat, rows, flat, rows, flat, rows),
        check_vma=False,
    )
```

time: 988 us -> 367 us (0.37)
  waiting for transfers between devices: 375 us -> 0 us
  Pallas kernels: 0 us -> 338 us
  matrix products: 319 us -> 0 us
  blocking collectives: 125 us -> 0 us
  other arithmetic: 96 us -> 2.7 us
  local copies, waits for them, and re-layouts: 48.8 us -> 19.4 us
  between operations: 17 us -> 0.92 us
    reduce_scatter x4 -> x0, waiting for transfers between devices: 342 us -> none  [the longest x1 187 us: local(): lax.psum_scatter(grad_in_matrix, ('wide', 'narrow'), scatter_dimension=0,...]
    pallas_call x0 -> x1, Pallas kernels: none -> 338 us  [whole_layer(): pl.pallas_call(layer_kernel, out_shape=[sd((T, T), bf16), sd((T, T), bf16...]
    dot_general x24 -> x0, matrix products: 319 us -> none  [the longest x4 83.5 us: times_transposed(): lax.dot_general(left, right, (((1,), (1,)), ((), ())), preferred_element_...]
    unnamed x2 -> x0, blocking collectives: 84.4 us -> none
    convert_element_type x10 -> x1, other arithmetic: 49.9 us -> 0.6 us  [local(): jnp.stack([row0, row1, fc_in_bias] + [jnp.zeros_like(row0)] * 5).astype(f32)]
    all_gather x1 -> x0, blocking collectives: 40.7 us -> none  [local(): lax.all_gather(shards[7], ('wide', 'narrow'), axis=0, tiled=True)]
    reduce_sum x7 -> x0, other arithmetic: 35 us -> none  [the longest x2 25.5 us: local(): totals = jnp.sum(expo, axis=-1, keepdims=True)]
    all_gather x4 -> x0, waiting for transfers between devices: 30.5 us -> none  [the longest x1 30.5 us: local(): lax.all_gather(shards[2], ('wide', 'narrow'), axis=0, tiled=True)]
  transfers between devices with their start and end apart: 8 -> 0, of which waited for: 3 -> 0; matrix products, arithmetic and copies ran while one was open for 46% -> 0% of each run, Pallas kernels for 0% -> 0%
where the time goes in v2:
time: 367 us; the launch traced here: 361 us
  Pallas kernels  338 us (92%)
  local copies, waits for them, and re-layouts  19.4 us (5%)
    pallas_call x1, Pallas kernels, whole_layer(): pl.pallas_call(layer_kernel, out_shape=[sd((T, T), bf16), sd((T, T), bf16...  338 us
    unnamed x17, local copies, waits for them, and re-layouts  10.4 us

profile of v2, /device:TPU:0, one launch (start us, length us, event | category | flops | bytes accessed | tf_op | source)
XLA Modules:
  0.0 361.3 jit_solution(1435435386075745761)
XLA Ops:
  0.6 0.8 maximum_bitcast_fusion
  1.5 0.7 stack.19
  2.1 0.6 convert_element_type.5.small
  2.7 1.4 copy.28
  4.2 0.2 copy.29
  4.4 1.0 copy.30.fc_in
  5.4 338.3 %shard_map.228 = (bf16[1024,1024]{1,0:T(8,128)(2,1)}, bf16[1024,1024]{1,0:T(8,128)(2,1)}, f32[32,3072]{1,0:T(8,128)}, f32[32,1024]{1,0:T(8,128)}, f32[32,4096]{1...) custom-call(s32[1,4]{1,0:T(1,128)} %lens.1, ...), custom_call_target="tpu_custom_call" | custom-call | tf_op jit(solution)/shard_map/pallas_call | solution.py:765
  343.7 1.3 sqrt_reduce_fusion
  345.0 1.2 slice_bitcast_fusion.3
  346.2 1.2 slice_bitcast_fusion.1
  347.4 1.4 slice_bitcast_fusion
  348.8 1.6 copy.31
  350.5 1.6 copy.32
  352.1 3.1 copy.33
  355.2 0.0 copy-done.1
  355.2 1.3 copy.39
  356.5 1.0 copy-done
  357.5 1.3 copy.40
  358.8 0.0 copy-done.3
  358.8 0.7 copy.41
  359.6 0.0 copy-done.4
  359.6 0.7 copy.42
  360.3 0.0 copy-done.2
  360.3 0.8 copy.43
  (7 shorter events, 0.0 us)
Async XLA Ops:
  352.1 3.1 copy-start.1
  355.2 2.3 copy-start
  357.5 1.3 copy-start.3
  357.5 2.1 copy-start.4
  357.5 2.7 copy-start.2

commit v3 on v2

--- a/solution.py
+++ b/solution.py
@@ -1,3 +1,4 @@
+import itertools
 from functools import partial
 
 import jax
@@ -189,7 +190,8 @@
                 copy.wait_recv()
             part = self.part(*self.index(i - 1, self.p.me["zxyc".index(self.axes[i - 1])]))
             for buf in self.landing(i - 1):
-                part[...] = part[...] + buf[...]
+                for at in itertools.product(*(range(n) for n in buf.shape[:-2])):
+                    part[at] = part[at] + buf[at]
         for copy in self.copies(i):
             copy.start()
 
@@ -212,23 +214,22 @@
     return first
 
 
-def tables(ends, cos_ref, up_ref, down_ref):
+def tables(ends, cos_ref, sin_ref):
     t = lax.broadcasted_iota(jnp.int32, (T, 128), 0)
     d = lax.broadcasted_iota(jnp.int32, (T, 128), 1) % 64
     offset = (t - begins(ends, t)).astype(f32)
     freq = jnp.exp((d % 8).astype(f32) * (-2.0 / 16 * 9.210340371976184))
     angle = offset * freq
-    cos, sin = jnp.cos(angle), jnp.sin(angle)
-    cos_ref[...] = jnp.where(d < 16, cos, 1.0)
-    up_ref[...] = jnp.where(d < 8, -sin, 0.0)
-    down_ref[...] = jnp.where((d >= 8) & (d < 16), sin, 0.0)
-
-
-def turn(v, cos, up, down, sign):
+    cos_ref[...] = jnp.where(d < 16, jnp.cos(angle), 1.0)
+    sin_ref[...] = jnp.where(d < 16, jnp.where(d < 8, -1.0, 1.0) * jnp.sin(angle), 0.0)
+
+
+def turn(v, cos, sin, sign):
+    first = lax.broadcasted_iota(jnp.int32, cos.shape, 1) % 64 < 8
     out = []
     for i in range(2):
         w = v[:, 128 * i : 128 * (i + 1)]
-        r = pltpu.roll(w, 120, 1) * up + pltpu.roll(w, 8, 1) * down
+        r = jnp.where(first, pltpu.roll(w, 120, 1), pltpu.roll(w, 8, 1)) * sin
         out.append(w * cos + r if sign > 0 else w * cos - r)
     return jnp.concatenate(out, axis=1)
 
@@ -286,7 +287,7 @@
             doz = jnp.where(head_row == h, doT[:, cols].astype(f32) * inv, 0.0).astype(bf16)
             dp = dg(v_s[0:kk, :], doz, 1, 0)
             DS[0:kk, hc] = (E[0:kk, hc].astype(f32) * (dp - dot)).astype(bf16)
-            dqT[hr, cols] = dg(kT[hr, 0:kk], DS[0:kk, hc], 1, 0)
+            dqT[pl.ds(256 * qb + 64 * h, 64), :] = dg(kT[hr, 0:kk], DS[0:kk, hc], 1, 0)
             return doz.T
 
         doz = jnp.concatenate([head(h) for h in range(4)], axis=0)
@@ -303,7 +304,10 @@
     for i in range(T // R):
         rows = pl.ds(i * R, R)
         tb = [t[rows, :] for t in tabs]
-        dqkv[rows, 0:256] = turn(dqT[:, rows].T * 0.125, *tb, -1).astype(bf16)
+        dq = jnp.concatenate(
+            [dqT[R * i + 256 * b : R * i + 256 * (b + 1), :].T for b in range(R // 256)]
+        )
+        dqkv[rows, 0:256] = turn(dq * 0.125, *tb, -1).astype(bf16)
         dqkv[rows, 256:512] = turn(dk[rows, :] * LN2, *tb, -1).astype(bf16)
         dqkv[rows, 512:768] = dv[rows, :].astype(bf16)
 
@@ -346,8 +350,19 @@
     return centred * inverse, inverse
 
 
-NP = 3
-NR = 2
+def swap_blocks(tiles):
+    block = lax.broadcasted_iota(jnp.int32, tiles[0].shape, 1) // 16
+    out = []
+    for b in range(8):
+        tile = None
+        for a in range(8):
+            moved = tiles[a] if a == b else pltpu.roll(tiles[a], (16 * (a - b)) % 128, 1)
+            tile = moved if tile is None else jnp.where(block == a, moved, tile)
+        out.append(tile)
+    return out
+
+
+NP = 4
 
 
 def lanes(start, size):
@@ -355,12 +370,13 @@
 
 
 def layer_kernel(
-    lens, tokens, cot, qkv, out, fc_in, down, small,
+    lens, tokens, cot, qkv, out, fc_in, down,
+    v_gain, v_shift, v_out, v_down, v_qkv, v_in,
     mixed, tokens_grad, out_q, out_o, out_i, out_d, out_s, stats,
     ag_q, ag_o, ag_i, ag_d, ag_s,
-    hid, hidT, g, hgrad, attT, vecs, gvecs, wide_b, wide_g, sv,
-    cos, up, turn_down, wo, wq, wd, dqkv, q_s, k_s, v_s, qT, kT, vT, doT, E, DS, mlp, dqT,
-    part, r1, r2, r3, rz, part_s, s1, s2, s3, sz,
+    hid, g, hgrad, attT, vecs, gvecs, wide_b, wide_g, sv,
+    cos, sin, wo, wq, wd, dqkv, q_s, k_s, v_s, qT, kT, vT, doT, E, DS, mlp,
+    packed, mixed_in, part, r1, r2, r3, rz, part_s, s1, s2, s3, sz,
     own, io, fetch, send, recv, gsend, grecv,
 ):
     place = Place()
@@ -378,7 +394,8 @@
         )
 
     def gather_o():
-        return gather(4, [lambda *a, h=h: ag_o.at[a + (pl.ds(16 * h, 16),)] for h in range(2)])
+        views = [lambda *a, h=h: ag_o.at[a + (pl.ds(16 * h, 16),)] for h in range(2)]
+        return gather(4, views)
 
     def gather_m(j):
         return gather(5 + j, [lambda *a: ag_i.at[(j,) + a], lambda *a: ag_d.at[(j,) + a]])
@@ -395,8 +412,8 @@
                 place,
                 lambda *a, k=k: part.at[(k, n % NP) + a + (ALL, pl.ds(0, width))],
                 [
-                    b.at[(k, n % NR) + (ALL,) * d + (ALL, pl.ds(0, width))]
-                    for b, d in ((r1, 3), (r2, 2), (r3, 1), (rz, 1))
+                    b.at[(k, n % count) + (ALL,) * d + (ALL, pl.ds(0, width))]
+                    for b, d, count in ((r1, 3, 2), (r2, 2, 4), (r3, 1, 4), (rz, 1, 4))
                 ],
                 ("zxy", "zyx")[k],
                 lambda s, k=k: send.at[n, k, s],
@@ -413,22 +430,18 @@
                     :, 256 * j : 256 * (j + 1)
                 ]
 
-    def end_m(n):
-        totals = [array.total() for array in sums(n, 1024)]
-
-        @pl.when(n == 4)
-        def _():
-            for h in range(2):
-                out_o[pl.ds(16 * h, 16), :] = totals[h]
-
-        @pl.when(n > 4)
-        def _():
-            j = jnp.maximum(n - 5, 0)
-            for h in range(2):
-                out_i[pl.ds(16 * h, 16), lanes(512 * j, 512)] = totals[0][
-                    :, 512 * h : 512 * (h + 1)
-                ]
-            out_d[pl.ds(pl.multiple_of(16 * j, 16), 16), :] = totals[1]
+    def end_o():
+        totals = [array.total() for array in sums(4, 1024)]
+        for h in range(2):
+            out_o[pl.ds(16 * h, 16), :] = totals[h]
+
+    def end_m(j):
+        totals = [array.total() for array in sums(5 + j, 1024)]
+        for h in range(2):
+            out_i[pl.ds(16 * h, 16), lanes(512 * j, 512)] = totals[0][
+                :, 512 * h : 512 * (h + 1)
+            ]
+        out_d[pl.ds(pl.multiple_of(16 * j, 16), 16), :] = totals[1]
 
     own_copies = []
 
@@ -438,7 +451,6 @@
         own_copies.append(copy)
         return copy
 
-    own_copy(small, ag_s.at[me])
     for i in range(QG):
         for j in range(3):
             own_copy(
@@ -448,38 +460,53 @@
         if i == 0:
             own_copy(out, ag_o.at[me])
     for j in range(MC):
-        own_copy(fc_in.at[:, pl.ds(512 * j, 512)], ag_i.at[(j,) + me])
         own_copy(down.at[pl.ds(16 * j, 16)], ag_d.at[(j,) + me])
     load_x = pltpu.make_async_copy(tokens, attT, io.at[0])
     load_x.start()
     load_g = pltpu.make_async_copy(cot, g, io.at[1])
     load_g.start()
+    packed[...] = jnp.zeros_like(packed)
+    for i, vector in enumerate((v_gain, v_shift, v_out, v_down)):
+        packed[0:1, 32 * i : 32 * (i + 1)] = vector[...].astype(f32)
+    packed[1:2, 0:96] = v_qkv[...].astype(f32)
+    packed[2:3, :] = v_in[...].astype(f32)
+    own_s = pltpu.make_async_copy(packed, ag_s.at[me], io.at[2])
+    own_s.start()
     place.greet()
-    own_copies[0].wait()
+    own_s.wait()
     step(vectors, 0)
-    for copy in own_copies[1:5]:
+    for copy in own_copies[:4]:
         copy.wait()
     q0, o = gather_q(0), gather_o()
     step(q0, 0)
     step(o, 0)
-    for copy in own_copies[5:]:
-        copy.wait()
+    for t in range(4):
+        tiles = [fc_in[:, 128 * (8 * t + r) : 128 * (8 * t + r + 1)].astype(f32) for r in range(8)]
+        for j, tile in enumerate(swap_blocks(tiles)):
+            mixed_in[j, :, 128 * t : 128 * (t + 1)] = tile.astype(bf16)
+    for j in range(MC):
+        own_copy(mixed_in.at[j], ag_i.at[(j,) + me])
+    step(vectors, 1)
     ends = [lens[0, 0], lens[0, 0] + lens[0, 1], lens[0, 0] + lens[0, 1] + lens[0, 2]]
 
     def flag(b, qb):
         return 256 * b >= begins(ends, jnp.full((1, 256), 256 * qb, jnp.int32))
 
-    tables(ends, cos, up, turn_down)
-    step(vectors, 1)
+    tables(ends, cos, sin)
+    step(vectors, 2)
     step(q0, 1)
-    step(vectors, 2)
+    for copy in own_copies[4:]:
+        copy.wait()
     step(gather_q(1), 0)
+    step(o, 1)
     step(vectors, 3)
-    step(o, 1)
+    step(gather_m(0), 0)
     step(vectors, 4)
     load_s = pltpu.make_async_copy(ag_s, sv, io.at[2])
     load_s.start()
     step(q0, 2)
+    step(o, 2)
+    step(gather_m(1), 0)
     load_s.wait()
     rows = sv[...].reshape(32, 8, 128)
     row0, row1, row2 = (rows[:, i, :].astype(bf16) for i in range(3))
@@ -487,17 +514,14 @@
         vecs[i : i + 1, :] = from_ranks(row0, i, 1024)
     wide_b[0:1, 0:3072] = from_ranks(row1, "qkv", 3072)
     wide_b[1:2, :] = from_ranks(row2, "fc_in", 4096)
-    step(o, 2)
-    step(gather_m(0), 0)
-    step(gather_m(1), 0)
+    step(gather_q(1), 1)
+    step(gather_q(2), 0)
     step(q0, 3)
     load_x.wait()
     for i in range(4):
         rows = pl.ds(256 * i, 256)
         normed, _ = normalised(attT[rows, :].astype(f32))
-        h = (normed * vecs[0:1, :] + vecs[1:2, :]).astype(bf16)
-        hid[rows, :] = h
-        hidT[:, rows] = h.T
+        hid[rows, :] = (normed * vecs[0:1, :] + vecs[1:2, :]).astype(bf16)
     hgrad[...] = jnp.zeros_like(hgrad)
     step(q0, 4)
 
@@ -506,15 +530,16 @@
 
     fetch_q(0).start()
     step(o, 3)
+    step(gather_m(0), 1)
+    load_g.wait()
     step(o, 4)
     fetch_o = pltpu.make_async_copy(ag_o, wo, fetch.at[2])
     fetch_o.start()
-    load_g.wait()
     fetch_o.wait()
 
     bufs = (
         q_s, k_s, v_s, qT, kT, vT, doT, E, DS,
-        mlp.at[:, pl.ds(0, 256)], mlp.at[:, pl.ds(256, 256)], dqT,
+        mlp.at[:, pl.ds(0, 256)], mlp.at[:, pl.ds(256, 256)], mlp.at[:, pl.ds(512, 256)],
     )
 
     def attention_step(i, carry):
@@ -524,47 +549,48 @@
 
         @pl.when(more)
         def _():
-            step(gather_q(i + 1), 1)
-
-            @pl.when(i < QG - 2)
-            def _():
-                step(gather_q(i + 2), 0)
-
-        step(a, 1)
+            step(gather_q(i + 1), 2)
+            step(gather_m(2 * i + 2), 0)
 
         def pump(p):
             if p == 0:
-                step(b, 1)
 
                 @pl.when(before)
                 def _():
                     step(sums(i - 1, 768), 1)
 
+                step(b, 1)
+
                 @pl.when(more)
                 def _():
-                    step(gather_m(2 * i + 2), 0)
+                    step(gather_m(2 * i + 3), 0)
 
             elif p == 1:
+                step(a, 2)
+
+                @pl.when(i < QG - 2)
+                def _():
+                    step(gather_q(i + 2), 1)
+
+            elif p == 2:
 
                 @pl.when(more)
                 def _():
-                    step(gather_q(i + 1), 2)
-                    step(gather_m(2 * i + 3), 0)
-
-            elif p == 2:
-                step(a, 2)
+                    step(gather_q(i + 1), 3)
 
                 @pl.when(before)
                 def _():
                     step(sums(i - 1, 768), 2)
+                    step(gather_m(2 * i - 2), 4)
+                    step(gather_m(2 * i - 1), 4)
 
             elif p == 3:
-
-                @pl.when(more)
+                step(b, 2)
+
+                @pl.when(i < QG - 3)
                 def _():
-                    step(gather_q(i + 1), 3)
-
-                step(b, 2)
+                    step(gather_q(i + 3), 0)
+
             elif p == 4:
                 step(a, 3)
 
@@ -572,16 +598,14 @@
                 def _():
                     step(gather_q(i + 1), 4)
                     fetch_q(i + 1).start()
+                    step(gather_m(2 * i + 2), 1)
 
                 @pl.when(before)
                 def _():
                     step(sums(i - 1, 768), 3)
 
-            elif p == 5:
+            elif p == 6:
                 step(b, 3)
-            else:
-                step(a, 4)
-                step(b, 4)
 
                 @pl.when(before)
                 def _():
@@ -594,11 +618,11 @@
             return wide_b[0:1, lanes(1024 * j + 256 * i, 256)]
 
         attention_group(
-            flag, hid, g, W, wo[i].reshape(256, T), bias, (cos, up, turn_down), bufs,
+            flag, hid, g, W, wo[i].reshape(256, T), bias, (cos, sin), bufs,
             attT.at[pl.ds(pl.multiple_of(256 * i, 256), 256)], dqkv, pump,
         )
         for b_ in range(2):
-            v = dg(hidT[512 * b_ : 512 * (b_ + 1), :], dqkv[...], 1, 0).astype(bf16)
+            v = dg(hid[:, 512 * b_ : 512 * (b_ + 1)], dqkv[...], 0, 0).astype(bf16)
             v = v.reshape(2, 2, 2, 2, 2, 16, 768)
             for h in range(2):
                 part[h, i % NP, 2 * b_ : 2 * b_ + 2, :, :, :, :, 0:768] = v[:, :, :, :, h]
@@ -626,18 +650,16 @@
 
     for copy in fetch_m(0):
         copy.start()
-    step(sums(3, 768), 1)
     for b in range(2):
         v = dg(attT[512 * b : 512 * (b + 1), :], g[...], 1, 0).astype(bf16)
         v = v.reshape(2, 2, 2, 2, 2, 16, T)
         for h in range(2):
             part[h, 4 % NP, 2 * b : 2 * b + 2] = v[:, :, :, :, h]
+    step(sums(3, 768), 1)
     step(sums(4, 1024), 0)
-    step(sums(3, 768), 2)
-    step(sums(4, 1024), 1)
-    step(sums(3, 768), 3)
     mlp[...] = jnp.zeros_like(mlp)
-    end_q(3)
+    step(gather_m(MC - 2), 4)
+    step(gather_m(MC - 1), 4)
 
     act, pg = DS.at[:, pl.ds(0, 512)], DS.at[:, pl.ds(512, 512)]
 
@@ -659,15 +681,42 @@
             a, d = gelu_parts(pre)
             act[rows, :] = a.astype(bf16)
             pg[rows, :] = (dg(g[rows, :], w_down, 1, 1) * d).astype(bf16)
+            if b == 0:
+                step(sums(j + 4, 1024), 1)
         wide_g[1:2, lanes(512 * j, 512)] = jnp.sum(pg[...].astype(f32), axis=0, keepdims=True)
+
+        @pl.when(j == 0)
+        def _():
+            step(sums(3, 768), 2)
+
+        @pl.when(j == 1)
+        def _():
+            step(sums(3, 768), 3)
+
+        @pl.when(j == 2)
+        def _():
+            end_q(3)
+            step(sums(4, 1024), 3)
+
+        @pl.when(j == 3)
+        def _():
+            end_o()
+
+        @pl.when(j > 3)
+        def _():
+            end_m(j - 4)
+
+        @pl.when(j > 2)
+        def _():
+            step(sums(j + 2, 1024), 3)
 
         @pl.when(j > 0)
         def _():
-            end_m(j + 3)
+            step(sums(j + 3, 1024), 2)
 
         slot = (j + 5) % NP
         for b in range(2):
-            v = dg(hidT[512 * b : 512 * (b + 1), :], pg[...], 1, 0).astype(bf16)
+            v = dg(hid[:, 512 * b : 512 * (b + 1)], pg[...], 0, 0).astype(bf16)
             v = v.reshape(2, 2, 2, 2, 2, 16, 512)
             for h in range(2):
                 part[0, slot, 2 * b : 2 * b + 2, :, :, :, :, 512 * h : 512 * (h + 1)] = v[
@@ -676,13 +725,10 @@
             v = dg(act[:, 256 * b : 256 * (b + 1)], g[...], 0, 0).astype(bf16)
             part[1, slot, 2 * b : 2 * b + 2] = v.reshape(2, 2, 2, 2, 16, T)
         step(sums(j + 5, 1024), 0)
-        step(sums(j + 4, 1024), 2)
         for b in range(2):
             rows = pl.ds(512 * b, 512)
             mlp[rows, :] += dg(act[rows, :], w_down, 1, 0)
             hgrad[rows, :] += dg(pg[rows, :], w_in, 1, 1)
-        step(sums(j + 5, 1024), 1)
-        step(sums(j + 4, 1024), 3)
         return carry
 
     lax.fori_loop(0, MC, mlp_step, 0)
@@ -690,6 +736,10 @@
     last = MC + 4
     reload_x = pltpu.make_async_copy(tokens, hid, io.at[0])
     reload_x.start()
+    step(sums(last, 1024), 1)
+    step(sums(last - 1, 1024), 2)
+    step(sums(last - 2, 1024), 3)
+    end_m(MC - 4)
     reload_x.wait()
     for i in range(4):
         rows = pl.ds(256 * i, 256)
@@ -702,11 +752,11 @@
         n = h * vecs[0:1, :]
         d = n - jnp.mean(n, axis=-1, keepdims=True)
         d = d - normed * jnp.mean(n * normed, axis=-1, keepdims=True)
-        hidT[rows, :] = (up_g + inverse * d).astype(bf16)
-    put_tg = pltpu.make_async_copy(hidT, tokens_grad, io.at[1])
+        E[rows, :] = (up_g + inverse * d).astype(bf16)
+    put_tg = pltpu.make_async_copy(E, tokens_grad, io.at[1])
     put_tg.start()
     step(sums(last, 1024), 2)
-    end_m(jnp.int32(last - 1))
+    step(sums(last - 1, 1024), 3)
     row0 = sum(to_ranks(gvecs[min(k, 2) : min(k, 2) + 1, :], k, 1024) for k in range(4))
     row1 = to_ranks(wide_g[0:1, 0:3072], "qkv", 3072)
     row2 = to_ranks(wide_g[1:2, :], "fc_in", 4096)
@@ -719,8 +769,10 @@
         lambda s: send.at[13, 0, s], lambda s: recv.at[13, 0, s],
     )
     tiny.step(0)
+    end_m(MC - 3)
+    tiny.step(1)
     step(sums(last, 1024), 3)
-    tiny.step(1)
+    tiny.step(2)
     w_out = wo[...].reshape(T, T)
     squares = [jnp.zeros((1, T), f32)] * 3
     for i in range(4):
@@ -733,14 +785,14 @@
             s + jnp.sum(v * v, axis=0, keepdims=True) for s, v in zip(squares, (x, a, m))
         ]
         if i == 1:
-            tiny.step(2)
+            tiny.step(3)
     put_mixed = pltpu.make_async_copy(hid, mixed, io.at[0])
     put_mixed.start()
-    tiny.step(3)
     for i in range(3):
         total = jnp.sum(squares[i], axis=1, keepdims=True)
         stats[i : i + 1, :] = jnp.broadcast_to(total, (1, 128))
-    end_m(jnp.int32(last))
+    end_m(MC - 2)
+    end_m(MC - 1)
     out_s[...] = tiny.total()
     put_tg.wait()
     put_mixed.wait()
@@ -756,7 +808,7 @@
     lax.fori_loop(0, MC, close_m, 0)
 
 
-def whole_layer(lens, tokens, cot, qkv, out, fc_in, down, small):
+def whole_layer(lens, tokens, cot, qkv, out, fc_in, down, *vectors):
     any_ = pl.BlockSpec(memory_space=pl.ANY)
     vmem = pl.BlockSpec(memory_space=pltpu.VMEM)
     sd = jax.ShapeDtypeStruct
@@ -779,10 +831,11 @@
             sd((MC,) + ranks + (16, 1024), bf16),
             sd(ranks + (8, 128), f32),
         ],
-        in_specs=[pl.BlockSpec(memory_space=pltpu.SMEM)] + [any_] * 7,
+        in_specs=[pl.BlockSpec(memory_space=pltpu.SMEM)]
+        + [any_] * 2
+        + [vmem] * 10,
         out_specs=[any_] * 2 + [vmem] * 6 + [any_] * 5,
         scratch_shapes=[
-            pltpu.VMEM((T, T), bf16),
             pltpu.VMEM((T, T), bf16),
             pltpu.VMEM((T, T), bf16),
             pltpu.VMEM((T, T), f32),
@@ -792,7 +845,6 @@
             pltpu.VMEM((8, 4096), f32),
             pltpu.VMEM((8, 4096), f32),
             pltpu.VMEM(ranks + (8, 128), f32),
-            pltpu.VMEM((T, 128), f32),
             pltpu.VMEM((T, 128), f32),
             pltpu.VMEM((T, 128), f32),
             pltpu.VMEM(ranks + (32, 1024), bf16),
@@ -809,12 +861,13 @@
             pltpu.VMEM((T, T), bf16),
             pltpu.VMEM((T, T), bf16),
             pltpu.VMEM((T, T), f32),
-            pltpu.VMEM((256, T), f32),
+            pltpu.VMEM((8, 128), f32),
+            pltpu.VMEM((MC, 32, 512), bf16),
             pltpu.VMEM((2, NP) + ranks + (16, 1024), bf16),
-            pltpu.VMEM((2, NR, 4, 2, 2, 16, 1024), bf16),
-            pltpu.VMEM((2, NR, 4, 2, 16, 1024), bf16),
-            pltpu.VMEM((2, NR, 4, 16, 1024), bf16),
-            pltpu.VMEM((2, NR, 3, 16, 1024), bf16),
+            pltpu.VMEM((2, 2, 4, 2, 2, 16, 1024), bf16),
+            pltpu.VMEM((2, 4, 4, 2, 16, 1024), bf16),
+            pltpu.VMEM((2, 4, 4, 16, 1024), bf16),
+            pltpu.VMEM((2, 4, 3, 16, 1024), bf16),
             pltpu.VMEM(ranks + (8, 128), f32),
             pltpu.VMEM((4, 2, 2, 8, 128), f32),
             pltpu.VMEM((4, 2, 8, 128), f32),
@@ -831,7 +884,60 @@
         compiler_params=pltpu.CompilerParams(
             collective_id=0, has_side_effects=True, vmem_limit_bytes=63 * 2**20
         ),
-    )(lens, tokens, cot, qkv, out, fc_in, down, small)
+    )(lens, tokens, cot, qkv, out, fc_in, down, *vectors)
+
+
+def finish_kernel(
+    mixed, tokens_grad, q, o, i_, d, s, stats,
+    f_mixed, f_tokens, f_gain, f_shift, f_q, f_qb, f_o, f_ob, f_i, f_ib, f_d, f_db, f_rms,
+    held, sem,
+):
+    moves = []
+    for n, (a, b) in enumerate(((mixed, f_mixed), (tokens_grad, f_tokens))):
+        for k in range(4):
+            rows = pl.ds(256 * k, 256)
+            into = pltpu.make_async_copy(a.at[rows], held.at[n, rows], sem.at[n, k])
+            into.start()
+            moves.append((into, pltpu.make_async_copy(held.at[n, rows], b.at[rows], sem.at[n, k])))
+    for into, out in moves:
+        into.wait()
+        out.start()
+    f_q[...] = q[...]
+    f_o[...] = o[...]
+    f_d[...] = d[...]
+    for t in range(4):
+        tiles = [i_[:, 512 * j + 128 * t : 512 * j + 128 * (t + 1)] for j in range(MC)]
+        for r, tile in enumerate(swap_blocks(tiles)):
+            f_i[:, 128 * (8 * t + r) : 128 * (8 * t + r + 1)] = tile
+    f_gain[...] = s[0:1, 0:32]
+    f_shift[...] = s[0:1, 32:64]
+    f_ob[...] = s[0:1, 64:96]
+    f_db[...] = s[0:1, 96:128]
+    f_qb[...] = s[1:2, 0:96]
+    f_ib[...] = s[2:3, :]
+    lane = lax.broadcasted_iota(jnp.int32, (1, 128), 1)
+    mean = jnp.where(lane == 0, stats[0:1, :], jnp.where(lane == 1, stats[1:2, :], stats[2:3, :]))
+    f_rms[...] = jnp.sqrt(mean * (1.0 / (T * T)))[:, 0:3]
+    for _, out in moves:
+        out.wait()
+
+
+def finish(mixed, tokens_grad, q, o, i_, d, s, stats):
+    any_ = pl.BlockSpec(memory_space=pl.ANY)
+    vmem = pl.BlockSpec(memory_space=pltpu.VMEM)
+    sd = jax.ShapeDtypeStruct
+    return pl.pallas_call(
+        finish_kernel,
+        out_shape=[
+            sd((T, T), bf16), sd((T, T), bf16), sd((1, 32), f32), sd((1, 32), f32),
+            sd((32, 3072), f32), sd((1, 96), f32), sd((32, 1024), f32), sd((1, 32), f32),
+            sd((32, 4096), f32), sd((1, 128), f32), sd((128, 1024), f32), sd((1, 32), f32),
+            sd((1, 3), f32),
+        ],
+        in_specs=[any_] * 2 + [vmem] * 6,
+        out_specs=[any_] * 2 + [vmem] * 11,
+        scratch_shapes=[pltpu.VMEM((2, T, T), bf16), pltpu.SemaphoreType.DMA((2, 4))],
+    )(mixed, tokens_grad, q, o, i_, d, s, stats)
 
 
 def layer_math(
@@ -960,19 +1066,14 @@
     tokens, cotangent, seq_lens, norm_gain, norm_bias, qkv_weight, qkv_bias, out_weight,
     out_bias, fc_in_weight, fc_in_bias, fc_out_weight, fc_out_bias,
 ):
-    in_mixed = fc_in_weight.reshape(32, 32, MC, 16).transpose(0, 2, 1, 3).reshape(32, 4096)
-    row0 = jnp.concatenate([norm_gain, norm_bias, out_bias, fc_out_bias])
-    row1 = jnp.pad(qkv_bias, (0, 32))
-    small = jnp.stack([row0, row1, fc_in_bias] + [jnp.zeros_like(row0)] * 5).astype(f32)
-    mixed, tokens_grad, out_q, out_o, out_i, out_d, out_s, stats, *_ = whole_layer(
-        seq_lens, tokens, cotangent, qkv_weight, out_weight, in_mixed, fc_out_weight, small
-    )
-    out_i = out_i.reshape(32, MC, 32, 16).transpose(0, 2, 1, 3).reshape(32, 4096)
-    stream_rms = jnp.sqrt(stats[0:3, 0] / (tokens.shape[0] * tokens.shape[1]))[None, :]
-    return (
-        mixed, tokens_grad, out_s[0, :32], out_s[0, 32:64], out_q, out_s[1, :96], out_o,
-        out_s[0, 64:96], out_i, out_s[2], out_d, out_s[0, 96:], stream_rms,
-    )
+    vectors = (norm_gain, norm_bias, out_bias, fc_out_bias, qkv_bias, fc_in_bias)
+    results = whole_layer(
+        seq_lens, tokens, cotangent, qkv_weight, out_weight, fc_in_weight, fc_out_weight,
+        *(v[None, :] for v in vectors),
+    )
+    results = finish(*results[:8])
+    flat = (2, 3, 5, 7, 9, 11)
+    return tuple(r[0] if n in flat else r for n, r in enumerate(results))
 
 
 def solution(mesh):

time: 367 us -> 280 us (0.76)
  Pallas kernels: 338 us -> 274 us
  local copies, waits for them, and re-layouts: 19.4 us -> 0 us
    pallas_call x1, Pallas kernels: 338 us -> 268 us  [whole_layer(): pl.pallas_call(layer_kernel, out_shape=[sd((T, T), bf16), sd((T, T), bf16...]
    unnamed x17 -> x0, local copies, waits for them, and re-layouts: 10.4 us -> none
    pallas_call x0 -> x1, Pallas kernels: none -> 6.35 us  [finish(): pl.pallas_call(finish_kernel, out_shape=[sd((T, T), bf16), sd((T, T), bf1...]
    squeeze x3 -> x0, local copies, waits for them, and re-layouts: 3.81 us -> none  [the longest x1 1.42 us: local(): out_s[0, 96:]]
where the time goes in v3:
time: 280 us; the launch traced here: 275 us
  Pallas kernels  274 us (98%)
    pallas_call x1, Pallas kernels, whole_layer(): pl.pallas_call(layer_kernel, out_shape=[sd((T, T), bf16), sd((T, T), bf16...  268 us
    pallas_call x1, Pallas kernels, finish(): pl.pallas_call(finish_kernel, out_shape=[sd((T, T), bf16), sd((T, T), bf1...  6.35 us

profile of v3, /device:TPU:0, one launch (start us, length us, event | category | flops | bytes accessed | tf_op | source)
XLA Modules:
  0.0 274.9 jit_solution(10536600376953736673)
XLA Ops:
  0.6 267.7 %shard_map.228 = (bf16[1024,1024]{1,0:T(8,128)(2,1)}, bf16[1024,1024]{1,0:T(8,128)(2,1)}, f32[32,3072]{1,0:T(8,128)}, f32[32,1024]{1,0:T(8,128)}, f32[32,4096]{1...) custom-call(s32[1,4]{1,0:T(1,128)} %lens.1, ...), custom_call_target="tpu_custom_call" | custom-call | tf_op jit(solution)/shard_map/pallas_call | solution.py:817
  268.3 6.4 %shard_map.229 = (bf16[1024,1024]{1,0:T(8,128)(2,1)}, bf16[1024,1024]{1,0:T(8,128)(2,1)}, f32[1,32]{1,0:T(1,128)}, f32[1,32]{1,0:T(1,128)}, f32[32,3072]{1,0:T(8...) custom-call(bf16[1024,1024]{1,0:T(8,128)(2,1)} %get-tuple-element.34, ...), custom_call_target="tpu_custom_call" | custom-call | tf_op jit(solution)/shard_map/pallas_call | solution.py:929

commit v4 on v3

--- a/solution.py
+++ b/solution.py
@@ -254,7 +254,7 @@
     pump(0)
     for i in range(T // R):
         rows = pl.ds(i * R, R)
-        do = dg(g[rows, :], Wo, 1, 1).astype(bf16)
+        do = dg(g[rows, :], Wo(), 1, 1).astype(bf16)
         doT[:, rows] = do.T
     head_row = lax.broadcasted_iota(jnp.int32, (256, 256), 0) // 64
     head_lane = lax.broadcasted_iota(jnp.int32, (256, 256), 1) // 64
@@ -397,8 +397,12 @@
         views = [lambda *a, h=h: ag_o.at[a + (pl.ds(16 * h, 16),)] for h in range(2)]
         return gather(4, views)
 
-    def gather_m(j):
-        return gather(5 + j, [lambda *a: ag_i.at[(j,) + a], lambda *a: ag_d.at[(j,) + a]])
+    def gather_m(j, odd):
+        down_view = lambda *a: ag_d.at[(j,) + a]
+        if not odd:
+            return gather(5 + j, [lambda *a: ag_i.at[(j,) + a], down_view])
+        views = [lambda *a, h=h: ag_i.at[(j,) + a + (pl.ds(16 * h, 16),)] for h in range(2)]
+        return gather(5 + j, views + [down_view], ("zxy", "zyx", "xyz"))
 
     def step(arrays, i):
         for array in arrays:
@@ -479,7 +483,6 @@
         copy.wait()
     q0, o = gather_q(0), gather_o()
     step(q0, 0)
-    step(o, 0)
     for t in range(4):
         tiles = [fc_in[:, 128 * (8 * t + r) : 128 * (8 * t + r + 1)].astype(f32) for r in range(8)]
         for j, tile in enumerate(swap_blocks(tiles)):
@@ -493,20 +496,18 @@
         return 256 * b >= begins(ends, jnp.full((1, 256), 256 * qb, jnp.int32))
 
     tables(ends, cos, sin)
+    step(o, 0)
     step(vectors, 2)
     step(q0, 1)
     for copy in own_copies[4:]:
         copy.wait()
+    step(vectors, 3)
     step(gather_q(1), 0)
-    step(o, 1)
-    step(vectors, 3)
-    step(gather_m(0), 0)
     step(vectors, 4)
     load_s = pltpu.make_async_copy(ag_s, sv, io.at[2])
     load_s.start()
     step(q0, 2)
-    step(o, 2)
-    step(gather_m(1), 0)
+    step(o, 1)
     load_s.wait()
     rows = sv[...].reshape(32, 8, 128)
     row0, row1, row2 = (rows[:, i, :].astype(bf16) for i in range(3))
@@ -514,28 +515,26 @@
         vecs[i : i + 1, :] = from_ranks(row0, i, 1024)
     wide_b[0:1, 0:3072] = from_ranks(row1, "qkv", 3072)
     wide_b[1:2, :] = from_ranks(row2, "fc_in", 4096)
-    step(gather_q(1), 1)
-    step(gather_q(2), 0)
-    step(q0, 3)
     load_x.wait()
     for i in range(4):
         rows = pl.ds(256 * i, 256)
         normed, _ = normalised(attT[rows, :].astype(f32))
         hid[rows, :] = (normed * vecs[0:1, :] + vecs[1:2, :]).astype(bf16)
-    hgrad[...] = jnp.zeros_like(hgrad)
+        if i == 1:
+            step(q0, 3)
+            step(gather_m(0, False), 0)
+    step(o, 2)
+    step(gather_q(1), 1)
+    step(gather_m(1, True), 0)
+    step(gather_q(2), 0)
     step(q0, 4)
 
     def fetch_q(i):
         return pltpu.make_async_copy(ag_q.at[i], wq.at[i % 2], fetch.at[i % 2])
 
     fetch_q(0).start()
-    step(o, 3)
-    step(gather_m(0), 1)
+    hgrad[...] = jnp.zeros_like(hgrad)
     load_g.wait()
-    step(o, 4)
-    fetch_o = pltpu.make_async_copy(ag_o, wo, fetch.at[2])
-    fetch_o.start()
-    fetch_o.wait()
 
     bufs = (
         q_s, k_s, v_s, qT, kT, vT, doT, E, DS,
@@ -545,27 +544,45 @@
     def attention_step(i, carry):
         fetch_q(i).wait()
         more, before = i < QG - 1, i > 0
-        a, b = gather_m(2 * i), gather_m(2 * i + 1)
+        a, b = gather_m(2 * i, False), gather_m(2 * i + 1, True)
+        b, slow = b[:2], b[2:]
+
+        @pl.when(before)
+        def _():
+            step(slow, 2)
 
         @pl.when(more)
         def _():
-            step(gather_q(i + 1), 2)
-            step(gather_m(2 * i + 2), 0)
+            step(gather_m(2 * i + 2, False), 0)
 
         def pump(p):
             if p == 0:
 
+                @pl.when(i == 0)
+                def _():
+                    step(o, 3)
+                    step(gather_m(0, False), 1)
+                    step(o, 4)
+                    fetch_o = pltpu.make_async_copy(ag_o, wo, fetch.at[2])
+                    fetch_o.start()
+                    fetch_o.wait()
+                    step(gather_q(1), 2)
+
                 @pl.when(before)
                 def _():
                     step(sums(i - 1, 768), 1)
 
-                step(b, 1)
 
                 @pl.when(more)
                 def _():
-                    step(gather_m(2 * i + 3), 0)
+                    step(gather_m(2 * i + 3, True), 0)
 
             elif p == 1:
+
+                @pl.when(i == 0)
+                def _():
+                    step(gather_m(1, True), 1)
+
                 step(a, 2)
 
                 @pl.when(i < QG - 2)
@@ -574,6 +591,10 @@
 
             elif p == 2:
 
+                @pl.when(i == 0)
+                def _():
+                    step(slow, 2)
+
                 @pl.when(more)
                 def _():
                     step(gather_q(i + 1), 3)
@@ -581,12 +602,23 @@
                 @pl.when(before)
                 def _():
                     step(sums(i - 1, 768), 2)
-                    step(gather_m(2 * i - 2), 4)
-                    step(gather_m(2 * i - 1), 4)
+
+                @pl.when(i > 1)
+                def _():
+                    end_q(i - 2)
+
+                @pl.when(before)
+                def _():
+                    step(gather_m(2 * i - 2, False), 4)
+                    step(gather_m(2 * i - 1, True), 4)
 
             elif p == 3:
                 step(b, 2)
 
+                @pl.when(more)
+                def _():
+                    step(gather_m(2 * i + 3, True)[2:], 1)
+
                 @pl.when(i < QG - 3)
                 def _():
                     step(gather_q(i + 3), 0)
@@ -598,18 +630,24 @@
                 def _():
                     step(gather_q(i + 1), 4)
                     fetch_q(i + 1).start()
-                    step(gather_m(2 * i + 2), 1)
+                    step(gather_m(2 * i + 2, False), 1)
 
                 @pl.when(before)
                 def _():
                     step(sums(i - 1, 768), 3)
 
             elif p == 6:
+
+                @pl.when(i < QG - 2)
+                def _():
+                    step(gather_q(i + 2), 2)
+
+                @pl.when(more)
+                def _():
+                    step(gather_m(2 * i + 3, True)[:2], 1)
+
                 step(b, 3)
-
-                @pl.when(before)
-                def _():
-                    end_q(i - 1)
+                step(slow, 3)
 
         def W(j):
             return wq[i % 2, :, :, :, :, :, 256 * j : 256 * (j + 1)].reshape(T, 256)
@@ -618,7 +656,7 @@
             return wide_b[0:1, lanes(1024 * j + 256 * i, 256)]
 
         attention_group(
-            flag, hid, g, W, wo[i].reshape(256, T), bias, (cos, sin), bufs,
+            flag, hid, g, W, lambda: wo[i].reshape(256, T), bias, (cos, sin), bufs,
             attT.at[pl.ds(pl.multiple_of(256 * i, 256), 256)], dqkv, pump,
         )
         for b_ in range(2):
@@ -658,8 +696,8 @@
     step(sums(3, 768), 1)
     step(sums(4, 1024), 0)
     mlp[...] = jnp.zeros_like(mlp)
-    step(gather_m(MC - 2), 4)
-    step(gather_m(MC - 1), 4)
+    step(gather_m(MC - 2, False), 4)
+    step(gather_m(MC - 1, True), 4)
 
     act, pg = DS.at[:, pl.ds(0, 512)], DS.at[:, pl.ds(512, 512)]
 
@@ -691,6 +729,7 @@
 
         @pl.when(j == 1)
         def _():
+            end_q(2)
             step(sums(3, 768), 3)
 
         @pl.when(j == 2)
@@ -801,11 +840,11 @@
             array.close()
 
     def close_m(j, carry):
-        for array in gather_m(j):
+        for array in gather_m(2 * j, False) + gather_m(2 * j + 1, True):
             array.close()
         return carry
 
-    lax.fori_loop(0, MC, close_m, 0)
+    lax.fori_loop(0, MC // 2, close_m, 0)
 
 
 def whole_layer(lens, tokens, cot, qkv, out, fc_in, down, *vectors):
@@ -878,8 +917,8 @@
             dma((4,)),
             dma((14, 2, 6)),
             dma((14, 2, 6)),
-            dma((14, 2, 6)),
-            dma((14, 2, 6)),
+            dma((14, 3, 6)),
+            dma((14, 3, 6)),
         ],
         compiler_params=pltpu.CompilerParams(
             collective_id=0, has_side_effects=True, vmem_limit_bytes=63 * 2**20
@@ -890,25 +929,34 @@
 def finish_kernel(
     mixed, tokens_grad, q, o, i_, d, s, stats,
     f_mixed, f_tokens, f_gain, f_shift, f_q, f_qb, f_o, f_ob, f_i, f_ib, f_d, f_db, f_rms,
-    held, sem,
+    held, held_q, held_o, held_d, held_i, turned, sem,
 ):
+    count = iter(range(16))
+
+    def move(src, there, dst):
+        n = next(count)
+        into = pltpu.make_async_copy(src, there, sem.at[n])
+        into.start()
+        return into, pltpu.make_async_copy(there, dst, sem.at[n])
+
+    load_i = pltpu.make_async_copy(i_, held_i, sem.at[15])
+    load_i.start()
     moves = []
     for n, (a, b) in enumerate(((mixed, f_mixed), (tokens_grad, f_tokens))):
         for k in range(4):
             rows = pl.ds(256 * k, 256)
-            into = pltpu.make_async_copy(a.at[rows], held.at[n, rows], sem.at[n, k])
-            into.start()
-            moves.append((into, pltpu.make_async_copy(held.at[n, rows], b.at[rows], sem.at[n, k])))
-    for into, out in moves:
-        into.wait()
-        out.start()
-    f_q[...] = q[...]
-    f_o[...] = o[...]
-    f_d[...] = d[...]
+            moves.append(move(a.at[rows], held.at[n, rows], b.at[rows]))
+    moves += [move(q, held_q, f_q), move(o, held_o, f_o), move(d, held_d, f_d)]
+    load_i.wait()
     for t in range(4):
-        tiles = [i_[:, 512 * j + 128 * t : 512 * j + 128 * (t + 1)] for j in range(MC)]
+        tiles = [held_i[:, 512 * j + 128 * t : 512 * j + 128 * (t + 1)] for j in range(MC)]
         for r, tile in enumerate(swap_blocks(tiles)):
-            f_i[:, 128 * (8 * t + r) : 128 * (8 * t + r + 1)] = tile
+            turned[:, 128 * (8 * t + r) : 128 * (8 * t + r + 1)] = tile
+        for into, out in moves[3 * t : 3 * t + 3]:
+            into.wait()
+            out.start()
+    put_i = pltpu.make_async_copy(turned, f_i, sem.at[15])
+    put_i.start()
     f_gain[...] = s[0:1, 0:32]
     f_shift[...] = s[0:1, 32:64]
     f_ob[...] = s[0:1, 64:96]
@@ -918,6 +966,7 @@
     lane = lax.broadcasted_iota(jnp.int32, (1, 128), 1)
     mean = jnp.where(lane == 0, stats[0:1, :], jnp.where(lane == 1, stats[1:2, :], stats[2:3, :]))
     f_rms[...] = jnp.sqrt(mean * (1.0 / (T * T)))[:, 0:3]
+    put_i.wait()
     for _, out in moves:
         out.wait()
 
@@ -934,9 +983,17 @@
             sd((32, 4096), f32), sd((1, 128), f32), sd((128, 1024), f32), sd((1, 32), f32),
             sd((1, 3), f32),
         ],
-        in_specs=[any_] * 2 + [vmem] * 6,
-        out_specs=[any_] * 2 + [vmem] * 11,
-        scratch_shapes=[pltpu.VMEM((2, T, T), bf16), pltpu.SemaphoreType.DMA((2, 4))],
+        in_specs=[any_] * 6 + [vmem, vmem],
+        out_specs=[any_, any_, vmem, vmem, any_, vmem, any_, vmem, any_, vmem, any_, vmem, vmem],
+        scratch_shapes=[
+            pltpu.VMEM((2, T, T), bf16),
+            pltpu.VMEM((32, 3072), f32),
+            pltpu.VMEM((32, 1024), f32),
+            pltpu.VMEM((128, 1024), f32),
+            pltpu.VMEM((32, 4096), f32),
+            pltpu.VMEM((32, 4096), f32),
+            pltpu.SemaphoreType.DMA((16,)),
+        ],
     )(mixed, tokens_grad, q, o, i_, d, s, stats)
 
 

time: 280 us -> 273 us (0.975)
  Pallas kernels: 274 us -> 267 us
    pallas_call x1, Pallas kernels: 268 us -> 261 us  [whole_layer(): pl.pallas_call(layer_kernel, out_shape=[sd((T, T), bf16), sd((T, T), bf16...]
where the time goes in v4:
time: 273 us; the launch traced here: 268 us
  Pallas kernels  267 us (98%)
    pallas_call x1, Pallas kernels, whole_layer(): pl.pallas_call(layer_kernel, out_shape=[sd((T, T), bf16), sd((T, T), bf16...  261 us
    pallas_call x1, Pallas kernels, finish(): pl.pallas_call(finish_kernel, out_shape=[sd((T, T), bf16), sd((T, T), bf1...  5.85 us

profile of v4, /device:TPU:0, one launch (start us, length us, event | category | flops | bytes accessed | tf_op | source)
XLA Modules:
  0.0 267.7 jit_solution(1694079701943667980)
XLA Ops:
  0.6 260.9 %shard_map.228 = (bf16[1024,1024]{1,0:T(8,128)(2,1)}, bf16[1024,1024]{1,0:T(8,128)(2,1)}, f32[32,3072]{1,0:T(8,128)}, f32[32,1024]{1,0:T(8,128)}, f32[32,4096]{1...) custom-call(s32[1,4]{1,0:T(1,128)} %lens.1, ...), custom_call_target="tpu_custom_call" | custom-call | tf_op jit(solution)/shard_map/pallas_call | solution.py:856
  261.6 5.9 %shard_map.229 = (bf16[1024,1024]{1,0:T(8,128)(2,1)}, bf16[1024,1024]{1,0:T(8,128)(2,1)}, f32[1,32]{1,0:T(1,128)}, f32[1,32]{1,0:T(1,128)}, f32[32,3072]{1,0:T(8...) custom-call(bf16[1024,1024]{1,0:T(8,128)(2,1)} %get-tuple-element.34, ...), custom_call_target="tpu_custom_call" | custom-call | tf_op jit(solution)/shard_map/pallas_call | solution.py:978

commit v5 on v4

--- a/solution.py
+++ b/solution.py
@@ -794,20 +794,23 @@
         E[rows, :] = (up_g + inverse * d).astype(bf16)
     put_tg = pltpu.make_async_copy(E, tokens_grad, io.at[1])
     put_tg.start()
-    step(sums(last, 1024), 2)
-    step(sums(last - 1, 1024), 3)
-    row0 = sum(to_ranks(gvecs[min(k, 2) : min(k, 2) + 1, :], k, 1024) for k in range(4))
-    row1 = to_ranks(wide_g[0:1, 0:3072], "qkv", 3072)
-    row2 = to_ranks(wide_g[1:2, :], "fc_in", 4096)
-    for r in range(32):
-        part_s[r // 8, r // 4 % 2, r // 2 % 2, r % 2] = jnp.concatenate(
-            [row0[r : r + 1], row1[r : r + 1], row2[r : r + 1], jnp.zeros((5, 128), f32)]
-        )
+    @pl.when(place.z >= 0)
+    def _():
+        row0 = sum(to_ranks(gvecs[min(k, 2) : min(k, 2) + 1, :], k, 1024) for k in range(4))
+        row1 = to_ranks(wide_g[0:1, 0:3072], "qkv", 3072)
+        row2 = to_ranks(wide_g[1:2, :], "fc_in", 4096)
+        for r in range(32):
+            part_s[r // 8, r // 4 % 2, r // 2 % 2, r % 2] = jnp.concatenate(
+                [row0[r : r + 1], row1[r : r + 1], row2[r : r + 1], jnp.zeros((5, 128), f32)]
+            )
+
     tiny = Scatter(
         place, lambda *a: part_s.at[a], [s1, s2, s3, sz], "zxy",
         lambda s: send.at[13, 0, s], lambda s: recv.at[13, 0, s],
     )
     tiny.step(0)
+    step(sums(last, 1024), 2)
+    step(sums(last - 1, 1024), 3)
     end_m(MC - 3)
     tiny.step(1)
     step(sums(last, 1024), 3)

time: 273 us -> 270 us (0.989)
  Pallas kernels: 267 us -> 264 us
    pallas_call x1, Pallas kernels: 261 us -> 258 us  [whole_layer(): pl.pallas_call(layer_kernel, out_shape=[sd((T, T), bf16), sd((T, T), bf16...]
where the time goes in v5:
time: 270 us; the launch traced here: 265 us
  Pallas kernels  264 us (98%)
    pallas_call x1, Pallas kernels, whole_layer(): pl.pallas_call(layer_kernel, out_shape=[sd((T, T), bf16), sd((T, T), bf16...  258 us
    pallas_call x1, Pallas kernels, finish(): pl.pallas_call(finish_kernel, out_shape=[sd((T, T), bf16), sd((T, T), bf1...  5.85 us

profile of v5, /device:TPU:0, one launch (start us, length us, event | category | flops | bytes accessed | tf_op | source)
XLA Modules:
  0.0 264.7 jit_solution(3138264013786764923)
XLA Ops:
  0.6 258.0 %shard_map.228 = (bf16[1024,1024]{1,0:T(8,128)(2,1)}, bf16[1024,1024]{1,0:T(8,128)(2,1)}, f32[32,3072]{1,0:T(8,128)}, f32[32,1024]{1,0:T(8,128)}, f32[32,4096]{1...) custom-call(s32[1,4]{1,0:T(1,128)} %lens.1, ...), custom_call_target="tpu_custom_call" | custom-call | tf_op jit(solution)/shard_map/pallas_call | solution.py:859
  258.6 5.9 %shard_map.229 = (bf16[1024,1024]{1,0:T(8,128)(2,1)}, bf16[1024,1024]{1,0:T(8,128)(2,1)}, f32[1,32]{1,0:T(1,128)}, f32[1,32]{1,0:T(1,128)}, f32[32,3072]{1,0:T(8...) custom-call(bf16[1024,1024]{1,0:T(8,128)(2,1)} %get-tuple-element.34, ...), custom_call_target="tpu_custom_call" | custom-call | tf_op jit(solution)/shard_map/pallas_call | solution.py:981
